TPU v7x, 32 devices: a whole 2x2x4 slice. The times are simulated.
32 devices in a mesh: slab: 16 (over z, y, x), shot: 2 (over core).
Axes of the slice: x: 2, y: 2, z: 4, core: 2. Of those that a mesh axis runs over, the one named last changes fastest.
Arguments:
- pressure_init: float32 [4, 128, 32, 256], P('shot', 'slab'), may hold values from -6 to 6
- adjoint_init: float32 [4, 128, 32, 256], P('shot', 'slab'), may hold values from -1.5 to 1.5
- density: float32 [128, 32, 256], P('slab'), may hold values from 0.5 to 2
- speed: float32 [128, 32, 256], P('slab'), may hold values from 0.6 to 1.1
- admittance: float32 [128, 32, 256], P('slab'), may hold values from 0.05 to 0.5
- bound_mask: int32 [128, 32, 256], P('slab'), may hold values 0 or 1
- rec_cells: int32 [48, 32], P('slab'), may hold values from 0 to 65535, as said below
- rec_live: int32 [48], P('slab'), may hold values from 0 to 1, as said below
- encoder: float32 [32, 25], replicated, may hold values from -1 to 1
- target: float32 [48, 4, 2, 25], P('slab', 'shot'), may hold values from -6 to 6
Outputs:
- recording: float32 [48, 4, 2, 25], P('slab', 'shot')
- gradient: float32 [128, 32, 256], P('slab')
Inputs may be any that keep to these rules, and one draw needn't show every extreme that they name: `rec_live`: in each aligned group of four slabs the numbers of live slots are 3, 1, 0 and 0 in an order drawn from the seed; a slab's live slots come first. `rec_cells`: each slot's 32 capsule cells form a block of 2 x 4 x 4 cells (z, x, y) inside its own slab.
All inputs are finite; a program needn't handle non-finite values. No bound on the sum of `bound_mask` on one device may be relied on, other than what follows from the above.
Results may differ from a plain program's by a relative error of at most 0.00017.
Values sent between devices are 32-bit elements; how exact they have to be, the bound alone decides.
A program may use at most 64 MiB of HBM per device.

v0:
```python
import jax
import jax.numpy as jnp
from jax import lax
from jax.sharding import PartitionSpec as P


def from_behind(value, axis, steps):
    count = lax.axis_size(axis)
    leading, last = (max(0, -steps), min(count, count - steps))
    return lax.ppermute(value, axis, [(source, source + steps) for source in range(leading, last)])


def rise_local(values, along):
    widths = [(0, 0)] * values.ndim
    widths[along] = (0, 1)
    padded = jnp.pad(values, widths)
    return lax.slice_in_dim(padded, 1, values.shape[along] + 1, axis=along) - values


def fall_local(values, along):
    widths = [(0, 0)] * values.ndim
    widths[along] = (1, 0)
    padded = jnp.pad(values, widths)
    return values - lax.slice_in_dim(padded, 0, values.shape[along], axis=along)


def rise_depth(values):
    above = from_behind(values[:, :1], "slab", -1)
    return jnp.concatenate([values[:, 1:], above], axis=1) - values


def fall_depth(values):
    below = from_behind(values[:, -1:], "slab", 1)
    return values - jnp.concatenate([below, values[:, :-1]], axis=1)


def selectors(rec_cells, width_x, width_y, planes, z_offset):
    flat = rec_cells.reshape(-1)
    depth_index = flat // (width_x * width_y) + z_offset
    row_index = flat // width_y % width_x
    col_index = flat % width_y
    plane_index = depth_index * width_x + row_index
    plane_pick = (
        plane_index[:, None] == jnp.arange(planes * width_x, dtype=jnp.int32)[None, :]
    ).astype(jnp.float32)
    col_pick = (col_index[:, None] == jnp.arange(width_y, dtype=jnp.int32)[None, :]).astype(
        jnp.float32
    )
    return (plane_pick, col_pick)


def sample_cells(field, plane_pick, col_pick):
    shots = field.shape[0]
    folded = field.reshape(shots, -1, field.shape[3])
    by_column = jnp.einsum("szy,ry->szr", folded, col_pick, precision=lax.Precision.HIGHEST)
    return jnp.sum(by_column * jnp.transpose(plane_pick)[None], axis=1)


def place_cells(values, plane_pick, col_pick, shape):
    spread = values[:, :, None] * col_pick[None]
    placed = jnp.einsum("rz,sry->szy", plane_pick, spread, precision=lax.Precision.HIGHEST)
    return placed.reshape(shape)


def body(
    pressure_init,
    adjoint_init,
    density,
    speed,
    admittance,
    bound_mask,
    rec_cells,
    rec_live,
    encoder,
    target,
):
    steps = target.shape[2]
    shots = pressure_init.shape[0]
    slab_depth = pressure_init.shape[1]
    width_x = pressure_init.shape[2]
    width_y = pressure_init.shape[3]
    slot_count = rec_cells.shape[0]
    capsules = rec_cells.shape[1]
    field_shape = pressure_init.shape
    wall = bound_mask.astype(jnp.float32)
    vel_coef = 0.5 / density
    pres_coef = 0.5 * density * speed * speed
    damping = 1.0 - admittance * wall
    coefs = jnp.stack([vel_coef, pres_coef, damping])
    live = rec_live.astype(jnp.float32)[:, None, None]
    margin = 0
    pressure = pressure_init
    plane_front, col_front = selectors(rec_cells, width_x, width_y, slab_depth + 2 * margin, margin)
    vel_use = coefs[0]
    pres_use = coefs[1]
    damp_use = coefs[2]
    flow_x = jnp.zeros_like(pressure)
    flow_y = jnp.zeros_like(pressure)
    flow_z = jnp.zeros_like(pressure)
    saved = []
    misfit = []
    records = []
    for moment in range(steps):
        flow_x = flow_x - vel_use * rise_local(pressure, 2)
        flow_y = flow_y - vel_use * rise_local(pressure, 3)
        flow_z = flow_z - vel_use * rise_depth(pressure)
        before = pressure - pres_use * (
            fall_local(flow_x, 2) + fall_local(flow_y, 3) + fall_depth(flow_z)
        )
        pressure = before * damp_use
        saved.append(before)
        sampled = sample_cells(pressure, plane_front, col_front).reshape(
            shots, slot_count, capsules
        )
        encoded = (
            jnp.einsum("src,ck->rsk", sampled, encoder, precision=lax.Precision.HIGHEST) * live
        )
        records.append(encoded)
        misfit.append(encoded - target[:, :, moment, :] * live)
    recording = jnp.stack(records, axis=2)
    sources = [
        jnp.einsum("rsk,ck->src", misfit[moment], encoder, precision=lax.Precision.HIGHEST).reshape(
            shots, -1
        )
        for moment in range(steps)
    ]
    plane_own, col_own = selectors(rec_cells, width_x, width_y, slab_depth, 0)
    adjoint = adjoint_init
    vel_back = coefs[0]
    pres_back = coefs[1]
    damp_back = coefs[2]
    back_x = jnp.zeros_like(adjoint)
    back_y = jnp.zeros_like(adjoint)
    back_z = jnp.zeros_like(adjoint)
    partial_grad = jnp.zeros(density.shape, jnp.float32)
    for moment in reversed(range(steps)):
        adjoint = adjoint + place_cells(sources[moment], plane_own, col_own, field_shape)
        inside = adjoint
        partial_grad = partial_grad - wall * jnp.sum(saved[moment] * inside, axis=0)
        if moment > 0:
            scaled = adjoint * damp_back
            weighted = pres_back * scaled
            back_x = back_x - rise_local(weighted, 2)
            back_y = back_y - rise_local(weighted, 3)
            back_z = back_z - rise_depth(weighted)
            adjoint = scaled - (
                fall_local(vel_back * back_x, 2)
                + fall_local(vel_back * back_y, 3)
                + fall_depth(vel_back * back_z)
            )
    shared = lax.psum_scatter(partial_grad, "shot", scatter_dimension=1, tiled=True)
    gradient = lax.all_gather(shared, "shot", axis=1, tiled=True)
    return (recording, gradient)


def solution(mesh):
    placed = (
        P("shot", "slab", None, None),
        P("shot", "slab", None, None),
        P("slab", None, None),
        P("slab", None, None),
        P("slab", None, None),
        P("slab", None, None),
        P("slab", None),
        P("slab"),
        P(),
        P("slab", "shot", None, None),
    )
    return jax.shard_map(
        body,
        mesh=mesh,
        in_specs=placed,
        out_specs=(P("slab", "shot", None, None), P("slab", None, None)),
        check_vma=False,
    )
```

profile of v0, /device:TPU:0, one launch (start us, length us, event | category | flops | bytes accessed | tf_op | source)
XLA Modules:
  0.0 77.8 jit_solution(12602208080775641663)
XLA Ops:
  7.2 0.0 copy-start
  7.2 0.0 copy-start.10
  7.2 0.0 reduce-scatter.2.cloned.1.call-start
  7.2 0.8 %slice.83 = f32[2,1,32,256]{3,2,1,0:T(8,128)S(1)} slice(f32[2,8,32,256]{3,2,1,0:T(8,128)} %param.10), slice={[0:2], [0:1], [0:32], [0:256]} | slice | bytes 131072 | tf_op jit(solution)/shard_map/slice | solution.py:28
  8.1 1.3 %collective-permute-start = (f32[2,1,32,256]{3,2,1,0:T(8,128)S(1)}, f32[2,1,32,256]{3,2,1,0:T(8,128)S(1)}, u32[]{:S(2)}, u32[]{:S(2)}) collective-permute-start(f32[2,1,32,256]{3,2,1,0:T(8,128)S(1)} %slice.83), channel_id=1, source_target_pairs={{2,0},{4,2},{6,4},{8,6},{10,8},{12,10},{14,12},{16,14},{18,16},{20... | collective-permute-start | bytes 196616 | tf_op jit(solution)/shard_map/ppermute | solution.py:10
  9.4 0.0 copy-done.10
  9.4 0.1 reshape.146
  9.5 0.1 fusion.58
  9.6 0.0 copy-start.6
  9.6 0.0 copy-start.4
  9.6 0.0 copy-start.8
  9.6 1.1 %multiply_multiply_fusion.1 = (f32[8,32,256]{2,1,0:T(8,128)S(1)}, f32[8,32,256]{2,1,0:T(8,128)S(1)}) fusion(f32[8,32,256]{2,1,0:T(8,128)} %param.13, f32[8,32,256]{2,1,0:T(8,128)} %param.12), kind=kLoop, calls=%fused_computation.72 | loop fusion | flops 262144 | bytes 1048576 | tf_op jit(solution)/shard_map/mul | solution.py:87
  10.8 0.0 copy-done.4
  10.8 0.0 copy-done.8
  10.9 0.0 copy-start.1
  10.9 0.1 fusion.54
  11.0 0.0 slice-start
  11.0 4.2 %collective-permute-done = f32[2,1,32,256]{3,2,1,0:T(8,128)S(1)} collective-permute-done((f32[2,1,32,256]{3,2,1,0:T(8,128)S(1)}, f32[2,1,32,256]{3,2,1,0:T(8,128)S(1)}, u32[]{:S(2)}, u32[]{:S(2)}) %collective-permute-start) | collective-permute-done | bytes 65568 | tf_op jit(solution)/shard_map/ppermute | solution.py:10
  15.2 0.0 copy-done.1
  15.2 0.0 slice-done
  15.2 0.3 fusion.4
  15.4 0.0 copy-start.9
  15.5 0.0 copy-start.11
  15.5 4.8 %collective-permute-start.1 = (f32[2,1,32,256]{3,2,1,0:T(8,128)S(1)}, f32[2,1,32,256]{3,2,1,0:T(8,128)S(1)}, u32[]{:S(2)}, u32[]{:S(2)}) collective-permute-start(f32[2,1,32,256]{3,2,1,0:T(8,128)S(1)} %slice.104), channel_id=1, source_target_pairs={{0,2},{2,4},{4,6},{6,8},{8,10},{10,12},{12,14},{14,16},{16,18},{18... | collective-permute-start | bytes 196616 | tf_op jit(solution)/shard_map/ppermute | solution.py:10
  20.3 0.0 copy-done.9
  20.3 0.0 copy-done.11
  20.4 1.8 %collective-permute-done.1 = f32[2,1,32,256]{3,2,1,0:T(8,128)S(1)} collective-permute-done((f32[2,1,32,256]{3,2,1,0:T(8,128)S(1)}, f32[2,1,32,256]{3,2,1,0:T(8,128)S(1)}, u32[]{:S(2)}, u32[]{:S(2)}) %collective-permute-start.1) | collective-permute-done | bytes 65568 | tf_op jit(solution)/shard_map/ppermute | solution.py:10
  22.2 0.4 broadcast_multiply_fusion.1
  22.6 0.6 slice.107
  23.2 1.3 %collective-permute-start.2 = (f32[2,1,32,256]{3,2,1,0:T(8,128)}, f32[2,1,32,256]{3,2,1,0:T(8,128)}, u32[]{:S(2)}, u32[]{:S(2)}) collective-permute-start(f32[2,1,32,256]{3,2,1,0:T(8,128)} %slice.107), channel_id=1, source_target_pairs={{2,0},{4,2},{6,4},{8,6},{10,8},{12,10},{14,12},{16,14},{18,16},{20... | collective-permute-start | bytes 196616 | tf_op jit(solution)/shard_map/ppermute | solution.py:10
  24.5 0.0 copy-done.6
  24.5 0.5 fusion
  25.0 0.8 %slice.106 = f32[2,7,32,256]{3,2,1,0:T(8,128)} slice(f32[2,8,32,256]{3,2,1,0:T(8,128)S(1)} %get-tuple-element.10), slice={[0:2], [1:8], [0:32], [0:256]} | slice | bytes 917504 | tf_op jit(solution)/shard_map/slice | solution.py:29
  25.9 0.1 reshape.147
  25.9 4.1 %collective-permute-done.2 = f32[2,1,32,256]{3,2,1,0:T(8,128)} collective-permute-done((f32[2,1,32,256]{3,2,1,0:T(8,128)}, f32[2,1,32,256]{3,2,1,0:T(8,128)}, u32[]{:S(2)}, u32[]{:S(2)}) %collective-permute-start.2) | collective-permute-done | bytes 65568 | tf_op jit(solution)/shard_map/ppermute | solution.py:10
  30.1 1.5 %fusion.12 = (f32[2,8,32,256]{3,2,1,0:T(8,128)S(1)}, f32[2,8,32,256]{3,2,1,0:T(8,128)S(1)}, f32[2,8,32,256]{3,2,1,0:T(8,128)S(1)}) fusion(f32[2,8,32,256]{3,2,1,0:T(8,128)S(1)} %get-tuple-element.17, f32[2,8,32,256]{3,2,1,0:T(8,128)S(1)} %get-tuple-element.10, f32[8,32,256]{2,1,0:T(8,128)S(1)} %get-tuple-element.22, ...), kind=kLoop, calls=%fused_computation.30 | loop fusion | flops 1441792 | bytes 5242880 | tf_op jit(solution)/shard_map/sub | solution.py:104
  31.6 4.8 %collective-permute-start.3 = (f32[2,1,32,256]{3,2,1,0:T(8,128)S(1)}, f32[2,1,32,256]{3,2,1,0:T(8,128)S(1)}, u32[]{:S(2)}, u32[]{:S(2)}) collective-permute-start(f32[2,1,32,256]{3,2,1,0:T(8,128)S(1)} %slice.108), channel_id=1, source_target_pairs={{0,2},{2,4},{4,6},{6,8},{8,10},{10,12},{12,14},{14,16},{16,18},{18... | collective-permute-start | bytes 196616 | tf_op jit(solution)/shard_map/ppermute | solution.py:10
  36.4 0.0 copy-done
  36.4 0.2 convolution_multiply_fusion.3
  36.6 1.7 %collective-permute-done.3 = f32[2,1,32,256]{3,2,1,0:T(8,128)S(1)} collective-permute-done((f32[2,1,32,256]{3,2,1,0:T(8,128)S(1)}, f32[2,1,32,256]{3,2,1,0:T(8,128)S(1)}, u32[]{:S(2)}, u32[]{:S(2)}) %collective-permute-start.3) | collective-permute-done | bytes 65568 | tf_op jit(solution)/shard_map/ppermute | solution.py:10
  38.3 1.3 %broadcast_multiply_fusion = (f32[2,8,32,256]{3,2,1,0:T(8,128)S(1)}, f32[2,8,32,256]{3,2,1,0:T(8,128)}) fusion(f32[8,32,256]{2,1,0:T(8,128)S(1)} %multiply_subtract_fusion.1, f32[2,8,32,256]{3,2,1,0:T(8,128)S(1)} %get-tuple-element.20, f32[2,7,32,256]{3,2,1,0:T(8,128)S(1)} %slice.109, f32[2,1,32,256]{3,2,1,0:T(8,128)S(1)} %collective-permute-done.3, ...), kind=kLoop, calls=%fused_computation.74 | loop fusion | flops 1310720 | bytes 4194304 | tf_op jit(solution)/shard_map/mul | solution.py:110
  39.5 0.5 fusion.1
  40.0 0.1 reshape.149
  40.1 0.2 convolution_multiply_fusion.2
  40.3 0.2 convolution_bitcast_fusion.1
  40.5 0.1 mul.232
  40.6 0.0 copy-done.2
  40.6 0.5 multiply_multiply_fusion
  41.2 1.3 %collective-permute-start.4 = (f32[2,1,32,256]{3,2,1,0:T(8,128)S(1)}, f32[2,1,32,256]{3,2,1,0:T(8,128)S(1)}, u32[]{:S(2)}, u32[]{:S(2)}) collective-permute-start(f32[2,1,32,256]{3,2,1,0:T(8,128)S(1)} %slice.111), channel_id=1, source_target_pairs={{2,0},{4,2},{6,4},{8,6},{10,8},{12,10},{14,12},{16,14},{18,16},{20... | collective-permute-start | bytes 196616 | tf_op jit(solution)/shard_map/ppermute | solution.py:10
  42.5 0.2 convolution_bitcast_fusion
  42.7 0.1 mul.244
  42.8 4.8 %collective-permute-done.4 = f32[2,1,32,256]{3,2,1,0:T(8,128)S(1)} collective-permute-done((f32[2,1,32,256]{3,2,1,0:T(8,128)S(1)}, f32[2,1,32,256]{3,2,1,0:T(8,128)S(1)}, u32[]{:S(2)}, u32[]{:S(2)}) %collective-permute-start.4) | collective-permute-done | bytes 65568 | tf_op jit(solution)/shard_map/ppermute | solution.py:10
  47.7 0.2 fusion.20
  47.9 4.8 %collective-permute-start.5 = (f32[2,1,32,256]{3,2,1,0:T(8,128)S(1)}, f32[2,1,32,256]{3,2,1,0:T(8,128)S(1)}, u32[]{:S(2)}, u32[]{:S(2)}) collective-permute-start(f32[2,1,32,256]{3,2,1,0:T(8,128)S(1)} %slice.112), channel_id=1, source_target_pairs={{0,2},{2,4},{4,6},{6,8},{8,10},{10,12},{12,14},{14,16},{16,18},{18... | collective-permute-start | bytes 196616 | tf_op jit(solution)/shard_map/ppermute | solution.py:10
  52.8 0.5 fusion.46
  53.3 1.3 %collective-permute-done.5 = f32[2,1,32,256]{3,2,1,0:T(8,128)S(1)} collective-permute-done((f32[2,1,32,256]{3,2,1,0:T(8,128)S(1)}, f32[2,1,32,256]{3,2,1,0:T(8,128)S(1)}, u32[]{:S(2)}, u32[]{:S(2)}) %collective-permute-start.5) | collective-permute-done | bytes 65568 | tf_op jit(solution)/shard_map/ppermute | solution.py:10
  54.6 0.6 multiply_reduce_fusion
  55.3 0.3 copy-done.5
  55.6 0.8 multiply_subtract_fusion
  56.4 0.0 reduce-scatter.2.cloned.1.call-update
  56.4 0.6 copy.17
  57.0 11.0 %reduce-scatter.2.cloned.1.call-done = f32[8,16,256]{2,1,0:T(8,128)} async-done(((f32[8,32,256]{2,1,0:T(8,128)}), f32[8,16,256]{2,1,0:T(8,128)}) %reduce-scatter.2.cloned.1.call-update) | async-done | bytes 131088 | tf_op jit(solution)/shard_map/reduce_scatter | solution.py:151
  68.0 2.3 %all_gather.3 = f32[8,32,256]{2,1,0:T(8,128)S(1)} all-gather(f32[8,16,256]{2,1,0:T(8,128)} %reduce-scatter.2.cloned.1.call-done), channel_id=1, replica_groups=mesh['slab'=16,'shot'=2] {'shot'}, dimensions={1}, use_global_device_ids=true | all-gather | bytes 393216 | tf_op jit(solution)/shard_map/all_gather | solution.py:152
  70.3 0.7 copy.33
  (19 shorter events, 0.3 us)
Async XLA Ops:
  7.2 29.2 %copy-start = (f32[32,25]{1,0:T(8,128)S(1)}, f32[32,25]{1,0:T(8,128)}, u32[]{:S(2)}) copy-start(f32[32,25]{1,0:T(8,128)} %param.18) | copy-start | bytes 9604
  7.2 2.2 %copy-start.10 = (s32[3,32]{1,0:T(4,128)S(1)}, s32[3,32]{1,0:T(4,128)}, u32[]{:S(2)}) copy-start(s32[3,32]{1,0:T(4,128)} %param.16) | copy-start | bytes 1156
  7.2 60.8 %reduce-scatter.2.cloned.1.call-start = ((), (), s32[]{:S(2)}) async-start(), calls=%async_computation.1 | async-start | bytes 393216 | tf_op jit(solution)/shard_map/reduce_scatter | solution.py:151
  8.1 7.1 %collective-permute-start = (f32[2,1,32,256]{3,2,1,0:T(8,128)S(1)}, f32[2,1,32,256]{3,2,1,0:T(8,128)S(1)}, u32[]{:S(2)}, u32[]{:S(2)}) collective-permute-start(f32[2,1,32,256]{3,2,1,0:T(8,128)S(1)} %slice.83), channel_id=1, source_target_pairs={{2,0},{4,2},{6,4},{8,6},{10,8},{12,10},{14,12},{16,14},{18,16},{20... | collective-permute-start | bytes 196616 | tf_op jit(solution)/shard_map/ppermute | solution.py:10
  9.6 15.0 %copy-start.6 = (f32[256,96]{0,1:T(8,128)}, f32[256,96]{0,1:T(8,128)S(1)}, u32[]{:S(2)}) copy-start(f32[256,96]{0,1:T(8,128)S(1)} %fusion.58) | copy-start | bytes 294916
  9.6 1.2 %copy-start.4 = (s32[8,32,256]{2,1,0:T(8,128)S(1)}, s32[8,32,256]{2,1,0:T(8,128)}, u32[]{:S(2)}) copy-start(s32[8,32,256]{2,1,0:T(8,128)} %param.15) | copy-start | bytes 786436
  9.6 1.2 %copy-start.8 = (f32[8,32,256]{2,1,0:T(8,128)S(1)}, f32[8,32,256]{2,1,0:T(8,128)}, u32[]{:S(2)}) copy-start(f32[8,32,256]{2,1,0:T(8,128)} %param.14) | copy-start | bytes 786436
  10.9 4.3 %copy-start.1 = (f32[2,8,32,256]{3,2,1,0:T(8,128)S(1)}, f32[2,8,32,256]{3,2,1,0:T(8,128)}, u32[]{:S(2)}) copy-start(f32[2,8,32,256]{3,2,1,0:T(8,128)} %param.10) | copy-start | bytes 1572868
  11.0 4.2 %slice-start = ((f32[2,8,32,256]{3,2,1,0:T(8,128)}), f32[2,7,32,256]{3,2,1,0:T(8,128)S(1)}, s32[]{:S(2)}) async-start(f32[2,8,32,256]{3,2,1,0:T(8,128)} %param.10), calls=%async_computation.2 | async-start | bytes 917504 | tf_op jit(solution)/shard_map/slice | solution.py:29
  15.4 4.9 %copy-start.9 = (f32[3,2,2,25]{3,2,1,0:T(2,128)S(1)}, f32[3,2,2,25]{3,2,1,0:T(2,128)}, u32[]{:S(2)}) copy-start(f32[3,2,2,25]{3,2,1,0:T(2,128)} %param.19) | copy-start | bytes 3604
  15.5 4.9 %copy-start.11 = (s32[3]{0:T(128)S(1)}, s32[3]{0:T(128)}, u32[]{:S(2)}) copy-start(s32[3]{0:T(128)} %param.17) | copy-start | bytes 40
  15.5 6.7 %collective-permute-start.1 = (f32[2,1,32,256]{3,2,1,0:T(8,128)S(1)}, f32[2,1,32,256]{3,2,1,0:T(8,128)S(1)}, u32[]{:S(2)}, u32[]{:S(2)}) collective-permute-start(f32[2,1,32,256]{3,2,1,0:T(8,128)S(1)} %slice.104), channel_id=1, source_target_pairs={{0,2},{2,4},{4,6},{6,8},{8,10},{10,12},{12,14},{14,16},{16,18},{18... | collective-permute-start | bytes 196616 | tf_op jit(solution)/shard_map/ppermute | solution.py:10
  23.2 6.8 %collective-permute-start.2 = (f32[2,1,32,256]{3,2,1,0:T(8,128)}, f32[2,1,32,256]{3,2,1,0:T(8,128)}, u32[]{:S(2)}, u32[]{:S(2)}) collective-permute-start(f32[2,1,32,256]{3,2,1,0:T(8,128)} %slice.107), channel_id=1, source_target_pairs={{2,0},{4,2},{6,4},{8,6},{10,8},{12,10},{14,12},{16,14},{18,16},{20... | collective-permute-start | bytes 196616 | tf_op jit(solution)/shard_map/ppermute | solution.py:10
  31.6 6.7 %collective-permute-start.3 = (f32[2,1,32,256]{3,2,1,0:T(8,128)S(1)}, f32[2,1,32,256]{3,2,1,0:T(8,128)S(1)}, u32[]{:S(2)}, u32[]{:S(2)}) collective-permute-start(f32[2,1,32,256]{3,2,1,0:T(8,128)S(1)} %slice.108), channel_id=1, source_target_pairs={{0,2},{2,4},{4,6},{6,8},{8,10},{10,12},{12,14},{14,16},{16,18},{18... | collective-permute-start | bytes 196616 | tf_op jit(solution)/shard_map/ppermute | solution.py:10
  38.3 1.3 %copy-start.7 = (f32[256,96]{0,1:T(8,128)S(1)}, f32[256,96]{0,1:T(8,128)}, u32[]{:S(2)}) copy-start(f32[256,96]{0,1:T(8,128)} %copy-done.6) | copy-start | bytes 294916
  39.5 1.1 %copy-start.2 = (f32[2,8,32,256]{3,2,1,0:T(8,128)S(1)}, f32[2,8,32,256]{3,2,1,0:T(8,128)}, u32[]{:S(2)}) copy-start(f32[2,8,32,256]{3,2,1,0:T(8,128)} %param.11) | copy-start | bytes 1572868
  41.2 6.5 %collective-permute-start.4 = (f32[2,1,32,256]{3,2,1,0:T(8,128)S(1)}, f32[2,1,32,256]{3,2,1,0:T(8,128)S(1)}, u32[]{:S(2)}, u32[]{:S(2)}) collective-permute-start(f32[2,1,32,256]{3,2,1,0:T(8,128)S(1)} %slice.111), channel_id=1, source_target_pairs={{2,0},{4,2},{6,4},{8,6},{10,8},{12,10},{14,12},{16,14},{18,16},{20... | collective-permute-start | bytes 196616 | tf_op jit(solution)/shard_map/ppermute | solution.py:10
  47.9 6.7 %collective-permute-start.5 = (f32[2,1,32,256]{3,2,1,0:T(8,128)S(1)}, f32[2,1,32,256]{3,2,1,0:T(8,128)S(1)}, u32[]{:S(2)}, u32[]{:S(2)}) collective-permute-start(f32[2,1,32,256]{3,2,1,0:T(8,128)S(1)} %slice.112), channel_id=1, source_target_pairs={{0,2},{2,4},{4,6},{6,8},{8,10},{10,12},{12,14},{14,16},{16,18},{18... | collective-permute-start | bytes 196616 | tf_op jit(solution)/shard_map/ppermute | solution.py:10
  53.3 1.4 %copy-start.3 = (f32[2,8,32,256]{3,2,1,0:T(8,128)S(1)}, f32[2,8,32,256]{3,2,1,0:T(8,128)}, u32[]{:S(2)}) copy-start(f32[2,8,32,256]{3,2,1,0:T(8,128)} %get-tuple-element.9) | copy-start | bytes 1572868
  54.6 1.0 %copy-start.5 = (s32[8,32,256]{2,1,0:T(8,128)S(1)}, s32[8,32,256]{2,1,0:T(8,128)}, u32[]{:S(2)}) copy-start(s32[8,32,256]{2,1,0:T(8,128)} %param.15) | copy-start | bytes 786436
Sparse Core Ops, SparseCore 0:
  56.5 11.4 reduce-scatter.1
where the time goes:
time: 78.3 us; the launch traced here: 77.8 us
  waiting for transfers between devices  29 us (37%)
  starting transfers between devices  18.3 us (23%)
  between operations  14.4 us (18%)
  other arithmetic  6.44 us (8%)
  local copies, waits for them, and re-layouts  4.61 us (6%)
  matrix products  2.77 us (4%)
  blocking collectives  2.29 us (3%)
    ppermute x6, starting transfers between devices, from_behind(): lax.ppermute(value, axis, [(source, source + steps) for source in range(l...  18.3 us
    ppermute x6, waiting for transfers between devices, from_behind(): lax.ppermute(value, axis, [(source, source + steps) for source in range(l...  18 us
    reduce_scatter x1, waiting for transfers between devices, body(): lax.psum_scatter(partial_grad, 'shot', scatter_dimension=1, tiled=True)  11 us
    all_gather x1, blocking collectives, body(): gradient = lax.all_gather(shared, 'shot', axis=1, tiled=True)  2.29 us
    sub x2, other arithmetic, body(): flow_x = flow_x - vel_use * rise_local(pressure, 2)  1.75 us
    unnamed x26, local copies, waits for them, and re-layouts  1.73 us
    mul x2, other arithmetic, body(): pressure = before * damp_use  1.7 us
  transfers between devices with their start and end apart: 7, of which 7 were waited for; matrix products, arithmetic and copies ran while one was open for 6% of the time, Pallas kernels for 0%

commit v1 on v0

v1 whole, which is shorter than its diff:
```python
import functools

import jax
import jax.numpy as jnp
from jax import lax
from jax.experimental import pallas as pl
from jax.experimental.pallas import tpu as pltpu
from jax.sharding import PartitionSpec as P

MESH = pl.DeviceIdType.MESH
F32 = jnp.float32


def split(value):
    high = value.astype(jnp.bfloat16)
    return high, (value - high.astype(F32)).astype(jnp.bfloat16)


def kernel(
    slabs,
    group,
    steps,
    slots,
    pressure_hbm,
    adjoint_hbm,
    density_hbm,
    speed_hbm,
    admittance_hbm,
    mask_hbm,
    cells_hbm,
    encoder_hbm,
    aux_hbm,
    record_hbm,
    grad_hbm,
    fields,
    weights,
    density,
    vel,
    pres,
    damp,
    mask,
    adjoint,
    before,
    after,
    placed,
    grads,
    total,
    cells,
    encoder,
    aux,
    record,
    load_sem,
    store_sem,
    send_sem,
    recv_sem,
    gsend_sem,
    grecv_sem,
):
    shots, depth, width_x, width_y = pressure_hbm.shape
    me = lax.axis_index("slab")
    mine = lax.axis_index("shot")
    has_below = me > 0
    has_above = me < slabs - 1

    inner = pl.ds(1, depth)
    pairs = [
        (density_hbm, density.at[inner]),
        (speed_hbm, pres),
        (admittance_hbm, damp),
        (mask_hbm, mask),
        (pressure_hbm, fields.at[0, :, inner]),
        (cells_hbm, cells),
        (encoder_hbm, encoder),
        (aux_hbm, aux),
        (adjoint_hbm, adjoint),
    ]
    loads = [pltpu.make_async_copy(a, b, load_sem.at[i]) for i, (a, b) in enumerate(pairs)]
    for load in loads:
        load.start()

    barrier = pltpu.get_barrier_semaphore()

    @pl.when(has_below)
    def _():
        pl.semaphore_signal(barrier, inc=1, device_id={"slab": me - 1}, device_id_type=MESH)

    @pl.when(has_above)
    def _():
        pl.semaphore_signal(barrier, inc=1, device_id={"slab": me + 1}, device_id_type=MESH)

    for j in range(1, group):
        pl.semaphore_signal(
            barrier, inc=1, device_id={"shot": lax.rem(mine + j, group)}, device_id_type=MESH
        )

    def halo(k, source, target, first, last):
        down = pltpu.make_async_remote_copy(
            src_ref=source.at[:, pl.ds(first, 1)],
            dst_ref=target.at[:, pl.ds(depth + 1, 1)],
            send_sem=send_sem.at[k, 0],
            recv_sem=recv_sem.at[k, 0],
            device_id={"slab": me - 1},
            device_id_type=MESH,
        )
        up = pltpu.make_async_remote_copy(
            src_ref=source.at[:, pl.ds(last, 1)],
            dst_ref=target.at[:, pl.ds(0, 1)],
            send_sem=send_sem.at[k, 1],
            recv_sem=recv_sem.at[k, 1],
            device_id={"slab": me + 1},
            device_id_type=MESH,
        )
        return down, up

    def start(pair):
        down, up = pair

        @pl.when(has_below)
        def _():
            down.start()

        @pl.when(has_above)
        def _():
            up.start()

    def arrive(pair):
        down, up = pair

        @pl.when(has_above)
        def _():
            down.wait_recv()

        @pl.when(has_below)
        def _():
            up.wait_recv()

    def sent(pair):
        down, up = pair

        @pl.when(has_below)
        def _():
            down.wait_send()

        @pl.when(has_above)
        def _():
            up.wait_send()

    rounds = [halo(0, pressure_hbm, fields.at[0], 0, depth - 1)]
    rounds += [halo(n, fields.at[n], fields.at[n], 1, depth) for n in range(1, steps)]
    rounds += [halo(steps + k, weights.at[k], weights.at[k], 1, depth) for k in range(steps - 1)]
    density_up = pltpu.make_async_remote_copy(
        src_ref=density_hbm.at[pl.ds(depth - 1, 1)],
        dst_ref=density.at[pl.ds(0, 1)],
        send_sem=send_sem.at[0, 2],
        recv_sem=recv_sem.at[0, 2],
        device_id={"slab": me + 1},
        device_id_type=MESH,
    )

    pl.semaphore_wait(
        barrier, has_below.astype(jnp.int32) + has_above.astype(jnp.int32) + (group - 1)
    )
    start(rounds[0])

    @pl.when(has_above)
    def _():
        density_up.start()

    zero = jnp.zeros((shots, width_x, width_y), F32)

    @pl.when(jnp.logical_not(has_below))
    def _():
        vel[0] = jnp.zeros((width_x, width_y), F32)
        for n in range(steps):
            fields[n, :, 0] = zero
        for k in range(steps - 1):
            weights[k, :, 0] = zero

    @pl.when(jnp.logical_not(has_above))
    def _():
        for n in range(steps):
            fields[n, :, depth + 1] = zero
        for k in range(steps - 1):
            weights[k, :, depth + 1] = zero

    rows = lax.broadcasted_iota(jnp.int32, (width_x, width_y), 0)
    cols = lax.broadcasted_iota(jnp.int32, (width_x, width_y), 1)

    def next_x(v):
        return jnp.where(rows == width_x - 1, 0.0, pltpu.roll(v, width_x - 1, 0))

    def next_y(v):
        return jnp.where(cols == width_y - 1, 0.0, pltpu.roll(v, width_y - 1, 1))

    def prev_x(v):
        return jnp.where(rows == 0, 0.0, pltpu.roll(v, 1, 0))

    def prev_y(v):
        return jnp.where(cols == 0, 0.0, pltpu.roll(v, 1, 1))

    def spread(ref, n, s, z):
        q = ref[n, s, z]
        v = vel[z]
        along_z = v * (ref[n, s, z + 1] - q) - vel[z - 1] * (q - ref[n, s, z - 1])
        along_x = v * (next_x(q) - q)
        along_y = v * (next_y(q) - q)
        return along_z + (along_x - prev_x(along_x)) + (along_y - prev_y(along_y))

    def forward(n, z):
        for s in range(shots):
            base = fields[0, s, z] if n == 0 else after[n - 1, s, z - 1]
            value = base + pres[z - 1] * spread(fields, n, s, z)
            before[n, s, z - 1] = value
            value = value * damp[z - 1]
            after[n, s, z - 1] = value
            if n + 1 < steps:
                fields[n + 1, s, z] = fields[n, s, z] + value

    def backward(n, z):
        k = steps - 1 - n
        part = jnp.zeros((width_x, width_y), F32)
        for s in range(shots):
            value = adjoint[s, z - 1] + placed[n, s, z - 1]
            if k > 0:
                value = value + spread(weights, k - 1, s, z)
            part = part + before[n, s, z - 1] * value
            if n > 0:
                scaled = value * damp[z - 1]
                adjoint[s, z - 1] = scaled
                weighted = pres[z - 1] * scaled
                if k > 0:
                    weighted = weighted + weights[k - 1, s, z]
                weights[k, s, z] = weighted
        if k > 0:
            part = grads[mine, z - 1] + part
        grads[mine, z - 1] = part

    def over(low, high, step):
        def run(z, carry):
            step(z)
            return carry

        lax.fori_loop(low, high, run, 0)

    edges = (1, depth)
    middle = tuple(range(2, depth))

    for load in loads[:4]:
        load.wait()

    def coefficients(z):
        rho = density[z]
        vel[z] = 0.5 / rho
        c = pres[z - 1]
        pres[z - 1] = 0.5 * rho * c * c
        damp[z - 1] = 1.0 - damp[z - 1] * mask[z - 1].astype(F32)

    over(1, depth + 1, coefficients)
    for load in loads[4:8]:
        load.wait()

    caps = encoder.shape[0]
    count = slots * caps
    flat = cells[...]
    plane_at = flat // width_y
    col_at = flat - plane_at * width_y
    pick_col = jnp.where(
        lax.broadcasted_iota(jnp.int32, (width_y, count), 0) == col_at, 1.0, 0.0
    ).astype(jnp.bfloat16)
    band = lax.broadcasted_iota(jnp.int32, (width_x, count), 0)

    def pick_plane(z):
        return band + (z - 1) * width_x == plane_at

    pad = record.shape[1]
    row_of = lax.broadcasted_iota(jnp.int32, (pad, count), 0)
    slot_of = lax.broadcasted_iota(jnp.int32, (pad, count), 1) // caps
    owns = [row_of == slot_of * shots + s for s in range(shots)]
    filters = jnp.concatenate([encoder[...]] * slots, axis=0)

    def sample(n, planes):
        highs, lows = [], []
        for s in range(shots):
            for z in planes:
                high, low = split(after[n, s, z - 1])
                highs.append(high)
                lows.append(low)
        got = jnp.dot(
            jnp.concatenate(highs + lows, axis=0), pick_col, preferred_element_type=F32
        )
        found = []
        at = 0
        half = len(highs) * width_x
        for s in range(shots):
            part = jnp.zeros((width_x, count), F32)
            for z in planes:
                value = got[at : at + width_x] + got[half + at : half + at + width_x]
                part = part + jnp.where(pick_plane(z), value, 0.0)
                at += width_x
            found.append(jnp.sum(part, axis=0, keepdims=True))
        return found

    def encode(n, found):
        table = jnp.zeros((pad, count), F32)
        for s in range(shots):
            table = jnp.where(owns[s], found[s], table)
        encoded = (
            jnp.dot(table, filters, precision=lax.Precision.HIGHEST, preferred_element_type=F32)
            * aux[steps]
        )
        record[n] = encoded
        wide = lax.dot_general(
            encoded - aux[n],
            filters,
            (((1,), (1,)), ((), ())),
            precision=lax.Precision.HIGHEST,
            preferred_element_type=F32,
        )
        return [
            jnp.sum(jnp.where(owns[s], wide, 0.0), axis=0, keepdims=True) for s in range(shots)
        ]

    def place(n, sources, planes):
        highs, lows = [], []
        for s in range(shots):
            high, low = split(sources[s])
            high, low = high.astype(F32), low.astype(F32)
            for z in planes:
                pick = pick_plane(z)
                highs.append(jnp.where(pick, high, 0.0).astype(jnp.bfloat16))
                lows.append(jnp.where(pick, low, 0.0).astype(jnp.bfloat16))
        put = lax.dot_general(
            jnp.concatenate(highs + lows, axis=0),
            pick_col,
            (((1,), (1,)), ((), ())),
            preferred_element_type=F32,
        )
        at = 0
        half = len(highs) * width_x
        for s in range(shots):
            for z in planes:
                placed[n, s, z - 1] = put[at : at + width_x] + put[half + at : half + at + width_x]
                at += width_x

    found = [None] * steps
    sources = [None] * steps
    for n in range(steps):
        over(2, depth, functools.partial(forward, n))
        if n > 0:
            found[n - 1] = sample(n - 1, middle + edges)
            sources[n - 1] = encode(n - 1, found[n - 1])
            place(n - 1, sources[n - 1], middle + edges)
        if n == steps - 1:
            inside = sample(n, middle)
        arrive(rounds[n])
        if n == 0:

            @pl.when(has_below)
            def _():
                density_up.wait_recv()
                vel[0] = 0.5 / density[0]

        for z in edges:
            forward(n, z)
        if n + 1 < steps:
            start(rounds[n + 1])

    last = steps - 1
    outside = sample(last, edges)
    sources[last] = encode(last, [a + b for a, b in zip(inside, outside)])
    loads[8].wait()
    record_store = pltpu.make_async_copy(record, record_hbm, store_sem.at[0])
    record_store.start()

    def share(k, low, size):
        planes = pl.ds(low, size)
        copies = []
        for j in range(1, group):
            copies.append(
                pltpu.make_async_remote_copy(
                    src_ref=grads.at[mine, planes],
                    dst_ref=grads.at[mine, planes],
                    send_sem=gsend_sem.at[k, j - 1],
                    recv_sem=grecv_sem.at[k, j - 1],
                    device_id={"shot": lax.rem(mine + j, group)},
                    device_id_type=MESH,
                )
            )
        return copies

    parts = [(1, depth - 2), (0, 1), (depth - 1, 1)]
    shares = [share(k, low, size) for k, (low, size) in enumerate(parts)]

    for n in reversed(range(steps)):
        k = last - n
        if k == 0:
            place(n, sources[n], edges)
            for z in edges:
                backward(n, z)
            if n > 0:
                start(rounds[steps])
            place(n, sources[n], middle)
            over(2, depth, functools.partial(backward, n))
        else:
            over(2, depth, functools.partial(backward, n))
            if n == 0:
                for copy in shares[0]:
                    copy.start()
            arrive(rounds[steps + k - 1])
            for z in edges:
                backward(n, z)
            if n > 0:
                start(rounds[steps + k])
    if steps == 1:
        for copy in shares[0]:
            copy.start()
    for copy in shares[1] + shares[2]:
        copy.start()

    stores = []
    for k, (low, size) in enumerate(parts):
        for copy in shares[k]:
            copy.wait_recv()
        planes = pl.ds(low, size)
        value = grads[0, planes]
        for t in range(1, group):
            value = value + grads[t, planes]
        total[planes] = value
        store = pltpu.make_async_copy(total.at[planes], grad_hbm.at[planes], store_sem.at[1 + k])
        store.start()
        stores.append(store)

    for pair in rounds:
        sent(pair)

    @pl.when(has_above)
    def _():
        density_up.wait_send()

    for copies in shares:
        for copy in copies:
            copy.wait_send()
    record_store.wait()
    for store in stores:
        store.wait()


def solution(mesh):
    slabs, group = mesh.shape["slab"], mesh.shape["shot"]

    def body(
        pressure_init,
        adjoint_init,
        density,
        speed,
        admittance,
        bound_mask,
        rec_cells,
        rec_live,
        encoder,
        target,
    ):
        shots, depth, width_x, width_y = pressure_init.shape
        slots, caps = rec_cells.shape
        steps, channels = target.shape[2], target.shape[3]
        count = slots * shots
        pad = -(-count // 8) * 8
        live = rec_live.astype(F32)[:, None, None, None]
        signals = jnp.transpose(target * live, (2, 0, 1, 3)).reshape(steps, count, channels)
        lives = jnp.broadcast_to(live, (slots, shots, 1, channels)).reshape(1, count, channels)
        aux = jnp.pad(
            jnp.concatenate([signals, lives], axis=0), ((0, 0), (0, pad - count), (0, 0))
        )
        plane = (depth, width_x, width_y)
        padded = (shots, depth + 2, width_x, width_y)
        any_spec = pl.BlockSpec(memory_space=pl.ANY)
        record, total = pl.pallas_call(
            functools.partial(kernel, slabs, group, steps, slots),
            out_shape=(
                jax.ShapeDtypeStruct((steps, pad, channels), F32),
                jax.ShapeDtypeStruct(plane, F32),
            ),
            in_specs=[any_spec] * 9,
            out_specs=(any_spec, any_spec),
            scratch_shapes=[
                pltpu.VMEM((steps,) + padded, F32),
                pltpu.VMEM((max(steps - 1, 1),) + padded, F32),
                pltpu.VMEM((depth + 1, width_x, width_y), F32),
                pltpu.VMEM((depth + 1, width_x, width_y), F32),
                pltpu.VMEM(plane, F32),
                pltpu.VMEM(plane, F32),
                pltpu.VMEM(plane, jnp.int32),
                pltpu.VMEM((shots,) + plane, F32),
                pltpu.VMEM((steps, shots) + plane, F32),
                pltpu.VMEM((steps, shots) + plane, F32),
                pltpu.VMEM((steps, shots) + plane, F32),
                pltpu.VMEM((group,) + plane, F32),
                pltpu.VMEM(plane, F32),
                pltpu.VMEM((1, slots * caps), jnp.int32),
                pltpu.VMEM((caps, channels), F32),
                pltpu.VMEM((steps + 1, pad, channels), F32),
                pltpu.VMEM((steps, pad, channels), F32),
                pltpu.SemaphoreType.DMA((9,)),
                pltpu.SemaphoreType.DMA((4,)),
                pltpu.SemaphoreType.DMA((2 * steps, 3)),
                pltpu.SemaphoreType.DMA((2 * steps, 3)),
                pltpu.SemaphoreType.DMA((3, max(group - 1, 1))),
                pltpu.SemaphoreType.DMA((3, max(group - 1, 1))),
            ],
            compiler_params=pltpu.CompilerParams(
                collective_id=0, has_side_effects=True, vmem_limit_bytes=40 * 1024 * 1024
            ),
        )(
            pressure_init,
            adjoint_init,
            density,
            speed,
            admittance,
            bound_mask,
            rec_cells.reshape(1, slots * caps),
            encoder,
            aux,
        )
        recording = jnp.transpose(
            record[:, :count].reshape(steps, slots, shots, channels), (1, 2, 0, 3)
        )
        gradient = -(bound_mask.astype(F32) * total)
        return recording, gradient

    placed = (
        P("shot", "slab", None, None),
        P("shot", "slab", None, None),
        P("slab", None, None),
        P("slab", None, None),
        P("slab", None, None),
        P("slab", None, None),
        P("slab", None),
        P("slab"),
        P(),
        P("slab", "shot", None, None),
    )
    return jax.shard_map(
        body,
        mesh=mesh,
        in_specs=placed,
        out_specs=(P("slab", "shot", None, None), P("slab", None, None)),
        check_vma=False,
    )
```

time: 78.3 us -> 30 us (0.38)
  waiting for transfers between devices: 29 us -> 0 us
  Pallas kernels: 0 us -> 19 us
  starting transfers between devices: 18.3 us -> 0 us
  between operations: 14.4 us -> 0.65 us
  other arithmetic: 6.44 us -> 1.49 us
  local copies, waits for them, and re-layouts: 4.61 us -> 8.19 us
  matrix products: 2.77 us -> 0 us
  blocking collectives: 2.29 us -> 0 us
    pallas_call x0 -> x1, Pallas kernels: none -> 19 us  [body(): pl.pallas_call(functools.partial(kernel, slabs, group, steps, slots), out...]
    ppermute x6 -> x0, starting transfers between devices: 18.3 us -> none  [from_behind(): lax.ppermute(value, axis, [(source, source + steps) for source in range(l...]
    ppermute x6 -> x0, waiting for transfers between devices: 18 us -> none  [from_behind(): lax.ppermute(value, axis, [(source, source + steps) for source in range(l...]
    reduce_scatter x1 -> x0, waiting for transfers between devices: 11 us -> none  [body(): lax.psum_scatter(partial_grad, 'shot', scatter_dimension=1, tiled=True)]
    unnamed x26 -> x16, local copies, waits for them, and re-layouts: 1.73 us -> 6.59 us
    mul x4 -> x1, other arithmetic: 3.08 us -> 0.07 us  [body(): target * live]
    dot_general x8 -> x0, matrix products: 2.77 us -> none  [the longest x2 1.02 us: place_cells(): jnp.einsum('rz,sry->szy', plane_pick, spread, precision=lax.Precision.HIG...]
    sub x4 -> x0, other arithmetic: 2.54 us -> none  [the longest x2 1.75 us: body(): flow_x = flow_x - vel_use * rise_local(pressure, 2)]
  transfers between devices with their start and end apart: 7 -> 0, of which waited for: 7 -> 0; matrix products, arithmetic and copies ran while one was open for 6% -> 0% of each run, Pallas kernels for 0% -> 0%
where the time goes in v1:
time: 30 us; the launch traced here: 29.4 us
  Pallas kernels  19 us (63%)
  local copies, waits for them, and re-layouts  8.19 us (27%)
  other arithmetic  1.49 us (5%)
  between operations  0.65 us (2%)
    pallas_call x1, Pallas kernels, body(): pl.pallas_call(functools.partial(kernel, slabs, group, steps, slots), out...  19 us
    unnamed x16, local copies, waits for them, and re-layouts  6.59 us
    reshape x1, local copies, waits for them, and re-layouts, body(): rec_cells.reshape(1, slots * caps)  0.78 us
    neg x1, other arithmetic, body(): gradient = -(bound_mask.astype(F32) * total)  0.75 us
    convert_element_type x1, other arithmetic, body(): live = rec_live.astype(F32)[:, None, None, None]  0.66 us

profile of v1, /device:TPU:0, one launch (start us, length us, event | category | flops | bytes accessed | tf_op | source)
XLA Modules:
  0.0 29.4 jit_solution(6364191497602139580)
XLA Ops:
  0.6 0.7 %convert_element_type.8 = f32[3]{0:T(128)S(1)} convert(s32[3]{0:T(128)} %param.17) | non-fusion elementwise | flops 3 | bytes 24 | tf_op jit(solution)/shard_map/convert_element_type | solution.py:468
  1.3 0.0 copy-start.7
  1.3 0.8 %reshape.17.cells_hbm = s32[1,96]{1,0:T(1,128)S(1)} reshape(s32[3,32]{1,0:T(4,128)} %param.16) | data formatting | bytes 768 | tf_op jit(solution)/shard_map/reshape | solution.py:520
  2.1 0.1 broadcast_in_dim.10
  2.1 0.1 broadcast_in_dim.11
  2.2 0.1 broadcast_in_dim.12
  2.3 0.0 copy-done.7
  2.3 0.1 broadcast_multiply_fusion
  2.4 0.0 copy-start.6
  2.4 0.7 %copy-done.6 = f32[32,25]{1,0:T(8,128)S(1)} copy-done((f32[32,25]{1,0:T(8,128)S(1)}, f32[32,25]{1,0:T(8,128)}, u32[]{:S(2)}) %copy-start.6) | copy-done | bytes 3224
  3.1 0.0 copy-start
  3.1 0.9 %copy-done = s32[8,32,256]{2,1,0:T(8,128)S(1)} copy-done((s32[8,32,256]{2,1,0:T(8,128)S(1)}, s32[8,32,256]{2,1,0:T(8,128)}, u32[]{:S(2)}) %copy-start) | copy-done | bytes 262168
  4.0 0.0 copy-start.1
  4.0 1.0 %copy-done.1 = f32[2,8,32,256]{3,2,1,0:T(8,128)S(1)} copy-done((f32[2,8,32,256]{3,2,1,0:T(8,128)S(1)}, f32[2,8,32,256]{3,2,1,0:T(8,128)}, u32[]{:S(2)}) %copy-start.1) | copy-done | bytes 524312
  5.1 0.0 copy-start.2
  5.1 1.0 %copy-done.2 = f32[2,8,32,256]{3,2,1,0:T(8,128)S(1)} copy-done((f32[2,8,32,256]{3,2,1,0:T(8,128)S(1)}, f32[2,8,32,256]{3,2,1,0:T(8,128)}, u32[]{:S(2)}) %copy-start.2) | copy-done | bytes 524312
  6.1 0.0 copy-start.3
  6.1 0.9 %copy-done.3 = f32[8,32,256]{2,1,0:T(8,128)S(1)} copy-done((f32[8,32,256]{2,1,0:T(8,128)S(1)}, f32[8,32,256]{2,1,0:T(8,128)}, u32[]{:S(2)}) %copy-start.3) | copy-done | bytes 262168
  7.1 0.0 copy-start.4
  7.1 0.9 %copy-done.4 = f32[8,32,256]{2,1,0:T(8,128)S(1)} copy-done((f32[8,32,256]{2,1,0:T(8,128)S(1)}, f32[8,32,256]{2,1,0:T(8,128)}, u32[]{:S(2)}) %copy-start.4) | copy-done | bytes 262168
  8.0 0.0 copy-start.5
  8.0 0.9 %copy-done.5 = f32[8,32,256]{2,1,0:T(8,128)S(1)} copy-done((f32[8,32,256]{2,1,0:T(8,128)S(1)}, f32[8,32,256]{2,1,0:T(8,128)}, u32[]{:S(2)}) %copy-start.5) | copy-done | bytes 262168
  9.0 19.0 %shard_map.113 = (f32[2,8,25]{2,1,0:T(8,128)S(1)}, f32[8,32,256]{2,1,0:T(8,128)S(1)}) custom-call(f32[2,8,32,256]{3,2,1,0:T(8,128)S(1)} %copy-done.1, f32[2,8,32,256]{3,2,1,0:T(8,128)S(1)} %copy-done.2, f32[8,32,256]{2,1,0:T(8,128)S(1)} %copy-done.3, f32[8,32,256]{2,1,0:T(8,128)S(1)} %copy-done.4, f32[8,32,256]{2,1,0:T(8,128)S(1)} %copy-done.5, ...), custom_call_target="tpu_custom_call" | custom-call | tf_op jit(solution)/shard_map/pallas_call | solution.py:477
  28.0 0.6 %copy.15 = f32[2,6,25]{2,0,1:T(2,128)} copy(f32[2,6,25]{2,1,0:T(8,128)S(1)} %bitcast.7) | data formatting | bytes 2400 | tf_op jit(solution)/shard_map/slice | solution.py:525
  28.6 0.7 %multiply_negate_fusion = f32[8,32,256]{2,1,0:T(8,128)} fusion(f32[8,32,256]{2,1,0:T(8,128)S(1)} %get-tuple-element.5, s32[8,32,256]{2,1,0:T(8,128)S(1)} %copy-done), kind=kLoop, calls=%fused_computation | loop fusion | flops 196608 | bytes 786432 | tf_op jit(solution)/shard_map/neg | solution.py:527
  (2 shorter events, 0.0 us)
Async XLA Ops:
  1.3 1.0 %copy-start.7 = (f32[3,2,2,25]{3,2,1,0:T(2,128)S(1)}, f32[3,2,2,25]{3,2,1,0:T(2,128)}, u32[]{:S(2)}) copy-start(f32[3,2,2,25]{3,2,1,0:T(2,128)} %param.19) | copy-start | bytes 3604
  2.4 0.7 %copy-start.6 = (f32[32,25]{1,0:T(8,128)S(1)}, f32[32,25]{1,0:T(8,128)}, u32[]{:S(2)}) copy-start(f32[32,25]{1,0:T(8,128)} %encoder_hbm.1) | copy-start | bytes 9604
  3.1 0.9 %copy-start = (s32[8,32,256]{2,1,0:T(8,128)S(1)}, s32[8,32,256]{2,1,0:T(8,128)}, u32[]{:S(2)}) copy-start(s32[8,32,256]{2,1,0:T(8,128)} %mask_hbm.1) | copy-start | bytes 786436
  4.0 1.0 %copy-start.1 = (f32[2,8,32,256]{3,2,1,0:T(8,128)S(1)}, f32[2,8,32,256]{3,2,1,0:T(8,128)}, u32[]{:S(2)}) copy-start(f32[2,8,32,256]{3,2,1,0:T(8,128)} %pressure_hbm.1) | copy-start | bytes 1572868
  5.1 1.0 %copy-start.2 = (f32[2,8,32,256]{3,2,1,0:T(8,128)S(1)}, f32[2,8,32,256]{3,2,1,0:T(8,128)}, u32[]{:S(2)}) copy-start(f32[2,8,32,256]{3,2,1,0:T(8,128)} %adjoint_hbm.1) | copy-start | bytes 1572868
  6.1 0.9 %copy-start.3 = (f32[8,32,256]{2,1,0:T(8,128)S(1)}, f32[8,32,256]{2,1,0:T(8,128)}, u32[]{:S(2)}) copy-start(f32[8,32,256]{2,1,0:T(8,128)} %density_hbm.1) | copy-start | bytes 786436
  7.1 0.9 %copy-start.4 = (f32[8,32,256]{2,1,0:T(8,128)S(1)}, f32[8,32,256]{2,1,0:T(8,128)}, u32[]{:S(2)}) copy-start(f32[8,32,256]{2,1,0:T(8,128)} %speed_hbm.1) | copy-start | bytes 786436
  8.0 0.9 %copy-start.5 = (f32[8,32,256]{2,1,0:T(8,128)S(1)}, f32[8,32,256]{2,1,0:T(8,128)}, u32[]{:S(2)}) copy-start(f32[8,32,256]{2,1,0:T(8,128)} %admittance_hbm.1) | copy-start | bytes 786436

commit v2 on v1

v2 whole, which is shorter than its diff:
```python
import functools

import jax
import jax.numpy as jnp
from jax import lax
from jax.experimental import pallas as pl
from jax.experimental.pallas import tpu as pltpu
from jax.sharding import PartitionSpec as P

MESH = pl.DeviceIdType.MESH
F32 = jnp.float32


def split(value):
    high = value.astype(jnp.bfloat16)
    return high, (value - high.astype(F32)).astype(jnp.bfloat16)


def kernel(
    slabs,
    group,
    steps,
    slots,
    pressure_hbm,
    adjoint_hbm,
    density_hbm,
    speed_hbm,
    admittance_hbm,
    mask_hbm,
    cells_hbm,
    live_hbm,
    encoder_hbm,
    target_hbm,
    record_hbm,
    grad_hbm,
    fields,
    weights,
    density,
    vel,
    pres,
    damp,
    mask,
    adjoint,
    before,
    after,
    placed,
    grads,
    total,
    cells,
    live,
    encoder,
    target,
    record,
    load_sem,
    store_sem,
    send_sem,
    recv_sem,
    gsend_sem,
    grecv_sem,
):
    shots, depth, width_x, width_y = pressure_hbm.shape
    me = lax.axis_index("slab")
    mine = lax.axis_index("shot")
    has_below = me > 0
    has_above = me < slabs - 1

    inner = pl.ds(1, depth)
    pairs = [
        (density_hbm, density.at[inner]),
        (speed_hbm, pres),
        (admittance_hbm, damp),
        (mask_hbm, mask),
        (pressure_hbm, fields.at[0, :, inner]),
        (cells_hbm, cells),
        (live_hbm, live),
        (encoder_hbm, encoder),
        (target_hbm, target),
        (adjoint_hbm, adjoint),
    ]
    loads = [pltpu.make_async_copy(a, b, load_sem.at[i]) for i, (a, b) in enumerate(pairs)]
    for load in loads:
        load.start()

    barrier = pltpu.get_barrier_semaphore()

    @pl.when(has_below)
    def _():
        pl.semaphore_signal(barrier, inc=1, device_id={"slab": me - 1}, device_id_type=MESH)

    @pl.when(has_above)
    def _():
        pl.semaphore_signal(barrier, inc=1, device_id={"slab": me + 1}, device_id_type=MESH)

    for j in range(1, group):
        pl.semaphore_signal(
            barrier, inc=1, device_id={"shot": lax.rem(mine + j, group)}, device_id_type=MESH
        )

    def halo(k, s, source, into, first, last):
        down = pltpu.make_async_remote_copy(
            src_ref=source.at[s, pl.ds(first, 1)],
            dst_ref=into.at[s, pl.ds(depth + 1, 1)],
            send_sem=send_sem.at[k, s, 0],
            recv_sem=recv_sem.at[k, s, 0],
            device_id={"slab": me - 1},
            device_id_type=MESH,
        )
        up = pltpu.make_async_remote_copy(
            src_ref=source.at[s, pl.ds(last, 1)],
            dst_ref=into.at[s, pl.ds(0, 1)],
            send_sem=send_sem.at[k, s, 1],
            recv_sem=recv_sem.at[k, s, 1],
            device_id={"slab": me + 1},
            device_id_type=MESH,
        )
        return down, up

    def start(pair):
        down, up = pair

        @pl.when(has_below)
        def _():
            down.start()

        @pl.when(has_above)
        def _():
            up.start()

    def arrive(pair):
        down, up = pair

        @pl.when(has_above)
        def _():
            down.wait_recv()

        @pl.when(has_below)
        def _():
            up.wait_recv()

    def sent(pair):
        down, up = pair

        @pl.when(has_below)
        def _():
            down.wait_send()

        @pl.when(has_above)
        def _():
            up.wait_send()

    each = range(shots)
    rounds = [[halo(0, s, pressure_hbm, fields.at[0], 0, depth - 1) for s in each]]
    for n in range(1, steps):
        rounds.append([halo(n, s, fields.at[n], fields.at[n], 1, depth) for s in each])
    for k in range(steps - 1):
        rounds.append(
            [halo(steps + k, s, weights.at[k], weights.at[k], 1, depth) for s in each]
        )
    density_up = pltpu.make_async_remote_copy(
        src_ref=density_hbm.at[pl.ds(depth - 1, 1)],
        dst_ref=density.at[pl.ds(0, 1)],
        send_sem=send_sem.at[0, 0, 2],
        recv_sem=recv_sem.at[0, 0, 2],
        device_id={"slab": me + 1},
        device_id_type=MESH,
    )

    pl.semaphore_wait(
        barrier, has_below.astype(jnp.int32) + has_above.astype(jnp.int32) + (group - 1)
    )

    @pl.when(has_above)
    def _():
        density_up.start()

    for s in each:
        start(rounds[0][s])

    zero = jnp.zeros((shots, width_x, width_y), F32)

    @pl.when(jnp.logical_not(has_below))
    def _():
        vel[0] = jnp.zeros((width_x, width_y), F32)
        for n in range(steps):
            fields[n, :, 0] = zero
        for k in range(steps - 1):
            weights[k, :, 0] = zero

    @pl.when(jnp.logical_not(has_above))
    def _():
        for n in range(steps):
            fields[n, :, depth + 1] = zero
        for k in range(steps - 1):
            weights[k, :, depth + 1] = zero

    rows = lax.broadcasted_iota(jnp.int32, (width_x, width_y), 0)
    cols = lax.broadcasted_iota(jnp.int32, (width_x, width_y), 1)

    def next_x(v):
        return jnp.where(rows == width_x - 1, 0.0, pltpu.roll(v, width_x - 1, 0))

    def next_y(v):
        return jnp.where(cols == width_y - 1, 0.0, pltpu.roll(v, width_y - 1, 1))

    def prev_x(v):
        return jnp.where(rows == 0, 0.0, pltpu.roll(v, 1, 0))

    def prev_y(v):
        return jnp.where(cols == 0, 0.0, pltpu.roll(v, 1, 1))

    def spread(ref, n, s, z):
        q = ref[n, s, z]
        v = vel[z]
        along_z = v * (ref[n, s, z + 1] - q) - vel[z - 1] * (q - ref[n, s, z - 1])
        along_x = v * (next_x(q) - q)
        along_y = v * (next_y(q) - q)
        return along_z + (along_x - prev_x(along_x)) + (along_y - prev_y(along_y))

    def forward(n, which, z):
        for s in which:
            base = fields[0, s, z] if n == 0 else after[n - 1, s, z - 1]
            value = base + pres[z - 1] * spread(fields, n, s, z)
            before[n, s, z - 1] = value
            value = value * damp[z - 1]
            after[n, s, z - 1] = value
            if n + 1 < steps:
                fields[n + 1, s, z] = fields[n, s, z] + value

    def backward(n, which, z):
        k = steps - 1 - n
        part = None if k == 0 and 0 in which else grads[mine, z - 1]
        for s in which:
            value = adjoint[s, z - 1] + placed[n, s, z - 1]
            if k > 0:
                value = value + spread(weights, k - 1, s, z)
            term = before[n, s, z - 1] * value
            part = term if part is None else part + term
            if n > 0:
                scaled = value * damp[z - 1]
                adjoint[s, z - 1] = scaled
                weighted = pres[z - 1] * scaled
                if k > 0:
                    weighted = weighted + weights[k - 1, s, z]
                weights[k, s, z] = weighted
        grads[mine, z - 1] = part

    def over(low, high, step):
        size = max(g for g in (1, 2, 3) if (high - low) % g == 0)

        def run(i, carry):
            for j in range(size):
                step(low + i * size + j)
            return carry

        lax.fori_loop(0, (high - low) // size, run, 0)

    edges = (1, depth)
    middle = tuple(range(2, depth))

    for load in loads[:4]:
        load.wait()

    def coefficients(z):
        rho = density[z]
        vel[z] = 0.5 / rho
        c = pres[z - 1]
        pres[z - 1] = 0.5 * rho * c * c
        damp[z - 1] = 1.0 - damp[z - 1] * mask[z - 1].astype(F32)

    over(1, depth + 1, coefficients)
    for load in loads[4:9]:
        load.wait()

    caps, channels = encoder.shape
    count = slots * caps
    lanes = -(-count // 128) * 128
    spare = lanes - count
    flat = [cells[pl.ds(r, 1), :] for r in range(slots)]
    if spare:
        flat.append(jnp.full((1, spare), -1, jnp.int32))
    flat = jnp.concatenate(flat, axis=1)
    plane_at = flat // width_y
    col_at = flat - plane_at * width_y
    pick_col = jnp.where(
        lax.broadcasted_iota(jnp.int32, (width_y, lanes), 0) == col_at, 1.0, 0.0
    ).astype(jnp.bfloat16)
    read_col = jnp.concatenate([pick_col, pick_col], axis=0)
    write_col = jnp.concatenate([pick_col, pick_col], axis=1)
    plane_twice = jnp.concatenate([plane_at, plane_at], axis=1)
    band = lax.broadcasted_iota(jnp.int32, (width_x, lanes), 0)
    band_twice = lax.broadcasted_iota(jnp.int32, (width_x, 2 * lanes), 0)

    pad = -(-slots * shots // 8) * 8
    slot_of = lax.broadcasted_iota(jnp.int32, (1, lanes), 1) // caps
    row_of = lax.broadcasted_iota(jnp.int32, (pad, lanes), 0)
    owns = [row_of == slot_of * shots + s for s in range(shots)]
    row_at = lax.broadcasted_iota(jnp.int32, (pad, channels), 0)
    live_row = jnp.zeros((pad, channels), F32)
    live_lane = jnp.zeros((1, lanes), F32)
    for r in range(slots):
        alive = live[r].astype(F32)
        live_row = jnp.where(row_at // shots == r, alive, live_row)
        live_lane = jnp.where(slot_of == r, alive, live_lane)
    filters = [encoder[...]] * slots
    if spare:
        filters.append(jnp.zeros((spare, channels), F32))
    filters = jnp.concatenate(filters, axis=0)

    def exact(a, b, contract):
        return lax.dot_general(
            a,
            b,
            (contract, ((), ())),
            precision=lax.Precision.HIGHEST,
            preferred_element_type=F32,
        )

    gram = exact(filters, filters, ((1,), (1,)))
    same = lax.broadcasted_iota(jnp.int32, (lanes, lanes), 0) // caps == slot_of
    gram_high, gram_low = split(jnp.where(same, gram, 0.0))
    gram = jnp.concatenate([gram_high, gram_high, gram_low], axis=0)

    goals = []
    for n in range(steps):
        signal = jnp.zeros((pad, channels), F32)
        for r in range(slots):
            for s in range(shots):
                signal = jnp.where(row_at == r * shots + s, target[r, s, pl.ds(n, 1), :], signal)
        wide = exact(signal * live_row, filters, ((1,), (1,)))
        goals.append(
            [
                jnp.sum(jnp.where(owns[s], wide, 0.0), axis=0, keepdims=True)
                for s in range(shots)
            ]
        )

    def sample(n, s, planes):
        values = jnp.concatenate([after[n, s, z - 1] for z in planes], axis=0)
        got = jnp.dot(
            jnp.concatenate(split(values), axis=1), read_col, preferred_element_type=F32
        )
        part = jnp.zeros((width_x, lanes), F32)
        for i, z in enumerate(planes):
            pick = band + (z - 1) * width_x == plane_at
            part = part + jnp.where(pick, got[i * width_x : (i + 1) * width_x], 0.0)
        return jnp.sum(part, axis=0, keepdims=True)

    def encode(n, found):
        table = jnp.zeros((pad, lanes), F32)
        for s in range(shots):
            table = jnp.where(owns[s], found[s], table)
        encoded = exact(table, filters, ((1,), (0,))) * live_row
        for r in range(slots):
            for s in range(shots):
                i = r * shots + s
                record[r, s, pl.ds(n, 1), :] = encoded[i : i + 1]

    def source(n, s, found):
        high, low = split(jnp.broadcast_to(found, (16, lanes)))
        wide = jnp.dot(
            jnp.concatenate([high, low, high], axis=1), gram, preferred_element_type=F32
        )
        return wide[0:1] * live_lane - goals[n][s]

    def place(n, s, value, planes):
        high, low = split(value)
        both = jnp.concatenate([high.astype(F32), low.astype(F32)], axis=1)
        spots = []
        for z in planes:
            pick = band_twice + (z - 1) * width_x == plane_twice
            spots.append(jnp.where(pick, both, 0.0).astype(jnp.bfloat16))
        put = lax.dot_general(
            jnp.concatenate(spots, axis=0),
            write_col,
            (((1,), (1,)), ((), ())),
            preferred_element_type=F32,
        )
        for i, z in enumerate(planes):
            placed[n, s, z - 1] = put[i * width_x : (i + 1) * width_x]

    last = steps - 1
    for n in range(steps):
        over(2, depth, functools.partial(forward, n, each))
        if n == last:
            found = [sample(n, s, middle) for s in each]
            loads[9].wait()
        if n == 0:

            @pl.when(has_below)
            def _():
                density_up.wait_recv()
                vel[0] = 0.5 / density[0]

        sources = []
        for s in each:
            arrive(rounds[n][s])
            for z in edges:
                forward(n, (s,), z)
            if n < last:
                start(rounds[n + 1][s])
            else:
                found[s] = found[s] + sample(n, s, edges)
                sources.append(source(n, s, found[s]))
                place(n, s, sources[s], edges)
                for z in edges:
                    backward(n, (s,), z)
                if n > 0:
                    start(rounds[steps][s])

    record_store = pltpu.make_async_copy(record, record_hbm, store_sem.at[0])

    def share(k, low, size):
        planes = pl.ds(low, size)
        copies = []
        for j in range(1, group):
            copies.append(
                pltpu.make_async_remote_copy(
                    src_ref=grads.at[mine, planes],
                    dst_ref=grads.at[mine, planes],
                    send_sem=gsend_sem.at[k, j - 1],
                    recv_sem=grecv_sem.at[k, j - 1],
                    device_id={"shot": lax.rem(mine + j, group)},
                    device_id_type=MESH,
                )
            )
        return copies

    parts = [(1, depth - 2), (0, 1), (depth - 1, 1)]
    shares = [share(k, low, size) for k, (low, size) in enumerate(parts)]

    for s in each:
        place(last, s, sources[s], middle)
    over(2, depth, functools.partial(backward, last, each))
    for n in reversed(range(last)):
        k = last - n
        old = [sample(n, s, middle + edges) for s in each]
        for s in each:
            place(n, s, source(n, s, old[s]), middle + edges)
        over(2, depth, functools.partial(backward, n, each))
        if n == 0:
            for copy in shares[0]:
                copy.start()
        encode(n, old)
        if n == 0:
            encode(last, found)
            record_store.start()
        for s in each:
            arrive(rounds[steps + k - 1][s])
            for z in edges:
                backward(n, (s,), z)
            if n > 0:
                start(rounds[steps + k][s])
    if steps == 1:
        encode(last, found)
        record_store.start()
        for copy in shares[0]:
            copy.start()
    for copy in shares[1] + shares[2]:
        copy.start()

    stores = []
    for k, (low, size) in enumerate(parts):
        for copy in shares[k]:
            copy.wait_recv()
        planes = pl.ds(low, size)
        value = grads[0, planes]
        for t in range(1, group):
            value = value + grads[t, planes]
        total[planes] = value
        store = pltpu.make_async_copy(total.at[planes], grad_hbm.at[planes], store_sem.at[1 + k])
        store.start()
        stores.append(store)

    for pairs in rounds:
        for pair in pairs:
            sent(pair)

    @pl.when(has_above)
    def _():
        density_up.wait_send()

    for copies in shares:
        for copy in copies:
            copy.wait_send()
    record_store.wait()
    for store in stores:
        store.wait()


def solution(mesh):
    slabs, group = mesh.shape["slab"], mesh.shape["shot"]

    def body(
        pressure_init,
        adjoint_init,
        density,
        speed,
        admittance,
        bound_mask,
        rec_cells,
        rec_live,
        encoder,
        target,
    ):
        shots, depth, width_x, width_y = pressure_init.shape
        slots, caps = rec_cells.shape
        steps, channels = target.shape[2], target.shape[3]
        plane = (depth, width_x, width_y)
        padded = (shots, depth + 2, width_x, width_y)
        any_spec = pl.BlockSpec(memory_space=pl.ANY)
        hbm_spec = any_spec
        record, total = pl.pallas_call(
            functools.partial(kernel, slabs, group, steps, slots),
            out_shape=(
                jax.ShapeDtypeStruct(target.shape, F32),
                jax.ShapeDtypeStruct(plane, F32),
            ),
            in_specs=[hbm_spec] * 10,
            out_specs=(any_spec, any_spec),
            scratch_shapes=[
                pltpu.VMEM((steps,) + padded, F32),
                pltpu.VMEM((max(steps - 1, 1),) + padded, F32),
                pltpu.VMEM((depth + 1, width_x, width_y), F32),
                pltpu.VMEM((depth + 1, width_x, width_y), F32),
                pltpu.VMEM(plane, F32),
                pltpu.VMEM(plane, F32),
                pltpu.VMEM(plane, jnp.int32),
                pltpu.VMEM((shots,) + plane, F32),
                pltpu.VMEM((steps, shots) + plane, F32),
                pltpu.VMEM((steps, shots) + plane, F32),
                pltpu.VMEM((steps, shots) + plane, F32),
                pltpu.VMEM((group,) + plane, F32),
                pltpu.VMEM(plane, F32),
                pltpu.VMEM((slots, caps), jnp.int32),
                pltpu.SMEM((slots,), jnp.int32),
                pltpu.VMEM((caps, channels), F32),
                pltpu.VMEM(target.shape, F32),
                pltpu.VMEM(target.shape, F32),
                pltpu.SemaphoreType.DMA((10,)),
                pltpu.SemaphoreType.DMA((4,)),
                pltpu.SemaphoreType.DMA((2 * steps, shots, 3)),
                pltpu.SemaphoreType.DMA((2 * steps, shots, 3)),
                pltpu.SemaphoreType.DMA((3, max(group - 1, 1))),
                pltpu.SemaphoreType.DMA((3, max(group - 1, 1))),
            ],
            compiler_params=pltpu.CompilerParams(
                collective_id=0, has_side_effects=True, vmem_limit_bytes=62 * 1024 * 1024
            ),
        )(
            pressure_init,
            adjoint_init,
            density,
            speed,
            admittance,
            bound_mask,
            rec_cells,
            rec_live,
            encoder,
            target,
        )
        gradient = -(bound_mask.astype(F32) * total)
        return record, gradient

    placed = (
        P("shot", "slab", None, None),
        P("shot", "slab", None, None),
        P("slab", None, None),
        P("slab", None, None),
        P("slab", None, None),
        P("slab", None, None),
        P("slab", None),
        P("slab"),
        P(),
        P("slab", "shot", None, None),
    )
    return jax.shard_map(
        body,
        mesh=mesh,
        in_specs=placed,
        out_specs=(P("slab", "shot", None, None), P("slab", None, None)),
        check_vma=False,
    )
```

time: 30 us -> 22.2 us (0.74)
  the two profiles are of different devices: /device:TPU:0 before, /device:TPU:25 now
where the time goes in v2:
time: 22.2 us; the launch traced here: 22.1 us
  Pallas kernels  19.1 us (86%)
  other arithmetic  1.69 us (8%)
  between operations  0.67 us (3%)
  local copies, waits for them, and re-layouts  0.6 us (3%)
    pallas_call x1, Pallas kernels, body(): pl.pallas_call(functools.partial(kernel, slabs, group, steps, slots), out...  19.1 us
    neg x1, other arithmetic, body(): gradient = -(bound_mask.astype(F32) * total)  1.69 us
    unnamed x5, local copies, waits for them, and re-layouts  0.6 us

profile of v2, /device:TPU:25, one launch (start us, length us, event | category | flops | bytes accessed | tf_op | source)
XLA Modules:
  0.0 22.1 jit_solution(6119650679432006916)
XLA Ops:
  0.6 0.0 copy-start
  0.6 19.1 %shard_map.113 = (f32[3,2,2,25]{3,2,1,0:T(2,128)}, f32[8,32,256]{2,1,0:T(8,128)}) custom-call(f32[2,8,32,256]{3,2,1,0:T(8,128)} %pressure_hbm.1, f32[2,8,32,256]{3,2,1,0:T(8,128)} %adjoint_hbm.1, f32[8,32,256]{2,1,0:T(8,128)} %density_hbm.1, f32[8,32,256]{2,1,0:T(8,128)} %speed_hbm.1, f32[8,32,256]{2,1,0:T(8,128)} %admittance_hbm.1, s32[8,32,256]{2,1,0:T(8,128)} %mask_hbm.1, ...), custom_call_target="tpu_custom_call" | custom-call | tf_op jit(solution)/shard_map/pallas_call | solution.py:512
  19.8 0.0 copy-done
  19.8 0.0 copy-start.1
  19.8 1.7 %multiply_negate_fusion = f32[8,32,256]{2,1,0:T(8,128)} fusion(f32[8,32,256]{2,1,0:T(8,128)} %get-tuple-element.5, s32[8,32,256]{2,1,0:T(8,128)S(1)} %copy-done), kind=kLoop, calls=%fused_computation | loop fusion | flops 196608 | bytes 786432 | tf_op jit(solution)/shard_map/neg | solution.py:561
  21.5 0.0 copy-done.1
  21.5 0.6 %copy.13 = f32[3,2,2,25]{3,2,1,0:T(2,128)} copy(f32[3,2,2,25]{3,2,1,0:T(2,128)S(1)} %copy-done.1) | data formatting | bytes 2400
Async XLA Ops:
  0.6 19.1 %copy-start = (s32[8,32,256]{2,1,0:T(8,128)S(1)}, s32[8,32,256]{2,1,0:T(8,128)}, u32[]{:S(2)}) copy-start(s32[8,32,256]{2,1,0:T(8,128)} %mask_hbm.1) | copy-start | bytes 786436
  19.8 1.7 %copy-start.1 = (f32[3,2,2,25]{3,2,1,0:T(2,128)S(1)}, f32[3,2,2,25]{3,2,1,0:T(2,128)}, u32[]{:S(2)}) copy-start(f32[3,2,2,25]{3,2,1,0:T(2,128)} %get-tuple-element.8) | copy-start | bytes 3604

commit v3 on v2

--- a/solution.py
+++ b/solution.py
@@ -31,12 +31,17 @@
     live_hbm,
     encoder_hbm,
     target_hbm,
-    record_hbm,
-    grad_hbm,
+    record,
+    total,
     fields,
     weights,
     density,
     vel,
+    next_x,
+    prev_x,
+    next_y,
+    prev_y,
+    centre,
     pres,
     damp,
     mask,
@@ -45,14 +50,11 @@
     after,
     placed,
     grads,
-    total,
     cells,
     live,
     encoder,
     target,
-    record,
     load_sem,
-    store_sem,
     send_sem,
     recv_sem,
     gsend_sem,
@@ -196,25 +198,12 @@
     rows = lax.broadcasted_iota(jnp.int32, (width_x, width_y), 0)
     cols = lax.broadcasted_iota(jnp.int32, (width_x, width_y), 1)
 
-    def next_x(v):
-        return jnp.where(rows == width_x - 1, 0.0, pltpu.roll(v, width_x - 1, 0))
-
-    def next_y(v):
-        return jnp.where(cols == width_y - 1, 0.0, pltpu.roll(v, width_y - 1, 1))
-
-    def prev_x(v):
-        return jnp.where(rows == 0, 0.0, pltpu.roll(v, 1, 0))
-
-    def prev_y(v):
-        return jnp.where(cols == 0, 0.0, pltpu.roll(v, 1, 1))
-
     def spread(ref, n, s, z):
         q = ref[n, s, z]
-        v = vel[z]
-        along_z = v * (ref[n, s, z + 1] - q) - vel[z - 1] * (q - ref[n, s, z - 1])
-        along_x = v * (next_x(q) - q)
-        along_y = v * (next_y(q) - q)
-        return along_z + (along_x - prev_x(along_x)) + (along_y - prev_y(along_y))
+        along_x = next_x[z] * pltpu.roll(q, width_x - 1, 0) + prev_x[z] * pltpu.roll(q, 1, 0)
+        along_y = next_y[z] * pltpu.roll(q, width_y - 1, 1) + prev_y[z] * pltpu.roll(q, 1, 1)
+        along_z = vel[z] * ref[n, s, z + 1] + vel[z - 1] * ref[n, s, z - 1]
+        return (along_x + along_y) + (along_z - centre[z] * q)
 
     def forward(n, which, z):
         for s in which:
@@ -262,12 +251,24 @@
 
     def coefficients(z):
         rho = density[z]
-        vel[z] = 0.5 / rho
+        v = 0.5 / rho
+        vel[z] = v
+        behind_x = jnp.where(rows == 0, 0.0, pltpu.roll(v, 1, 0))
+        behind_y = jnp.where(cols == 0, 0.0, pltpu.roll(v, 1, 1))
+        next_x[z] = jnp.where(rows == width_x - 1, 0.0, v)
+        next_y[z] = jnp.where(cols == width_y - 1, 0.0, v)
+        prev_x[z] = behind_x
+        prev_y[z] = behind_y
+        centre[z] = 3.0 * v + behind_x + behind_y
         c = pres[z - 1]
         pres[z - 1] = 0.5 * rho * c * c
         damp[z - 1] = 1.0 - damp[z - 1] * mask[z - 1].astype(F32)
 
+    def add_below(z):
+        centre[z] = centre[z] + vel[z - 1]
+
     over(1, depth + 1, coefficients)
+    over(2, depth + 1, add_below)
     for load in loads[4:9]:
         load.wait()
 
@@ -390,6 +391,7 @@
             def _():
                 density_up.wait_recv()
                 vel[0] = 0.5 / density[0]
+                add_below(1)
 
         sources = []
         for s in each:
@@ -407,8 +409,6 @@
                 if n > 0:
                     start(rounds[steps][s])
 
-    record_store = pltpu.make_async_copy(record, record_hbm, store_sem.at[0])
-
     def share(k, low, size):
         planes = pl.ds(low, size)
         copies = []
@@ -443,7 +443,6 @@
         encode(n, old)
         if n == 0:
             encode(last, found)
-            record_store.start()
         for s in each:
             arrive(rounds[steps + k - 1][s])
             for z in edges:
@@ -452,13 +451,11 @@
                 start(rounds[steps + k][s])
     if steps == 1:
         encode(last, found)
-        record_store.start()
         for copy in shares[0]:
             copy.start()
     for copy in shares[1] + shares[2]:
         copy.start()
 
-    stores = []
     for k, (low, size) in enumerate(parts):
         for copy in shares[k]:
             copy.wait_recv()
@@ -466,11 +463,7 @@
         value = grads[0, planes]
         for t in range(1, group):
             value = value + grads[t, planes]
-        total[planes] = value
-        store = pltpu.make_async_copy(total.at[planes], grad_hbm.at[planes], store_sem.at[1 + k])
-        store.start()
-        stores.append(store)
-
+        total[planes] = -(mask[planes].astype(F32) * value)
     for pairs in rounds:
         for pair in pairs:
             sent(pair)
@@ -482,9 +475,17 @@
     for copies in shares:
         for copy in copies:
             copy.wait_send()
-    record_store.wait()
-    for store in stores:
-        store.wait()
+
+
+def deliver(record, total, record_hbm, total_hbm, sem):
+    copies = [
+        pltpu.make_async_copy(total, total_hbm, sem.at[0]),
+        pltpu.make_async_copy(record, record_hbm, sem.at[1]),
+    ]
+    for copy in copies:
+        copy.start()
+    for copy in copies:
+        copy.wait()
 
 
 def solution(mesh):
@@ -508,18 +509,27 @@
         plane = (depth, width_x, width_y)
         padded = (shots, depth + 2, width_x, width_y)
         any_spec = pl.BlockSpec(memory_space=pl.ANY)
-        hbm_spec = any_spec
+        vmem_spec = pl.BlockSpec(memory_space=pltpu.VMEM)
+
+        def in_hbm(value):
+            return pltpu.with_memory_space_constraint(value, pltpu.HBM)
+
         record, total = pl.pallas_call(
             functools.partial(kernel, slabs, group, steps, slots),
             out_shape=(
-                jax.ShapeDtypeStruct(target.shape, F32),
-                jax.ShapeDtypeStruct(plane, F32),
+                pltpu.VMEM(target.shape, F32),
+                pltpu.VMEM(plane, F32),
             ),
-            in_specs=[hbm_spec] * 10,
-            out_specs=(any_spec, any_spec),
+            in_specs=[any_spec] * 10,
+            out_specs=(vmem_spec, vmem_spec),
             scratch_shapes=[
                 pltpu.VMEM((steps,) + padded, F32),
                 pltpu.VMEM((max(steps - 1, 1),) + padded, F32),
+                pltpu.VMEM((depth + 1, width_x, width_y), F32),
+                pltpu.VMEM((depth + 1, width_x, width_y), F32),
+                pltpu.VMEM((depth + 1, width_x, width_y), F32),
+                pltpu.VMEM((depth + 1, width_x, width_y), F32),
+                pltpu.VMEM((depth + 1, width_x, width_y), F32),
                 pltpu.VMEM((depth + 1, width_x, width_y), F32),
                 pltpu.VMEM((depth + 1, width_x, width_y), F32),
                 pltpu.VMEM(plane, F32),
@@ -530,36 +540,44 @@
                 pltpu.VMEM((steps, shots) + plane, F32),
                 pltpu.VMEM((steps, shots) + plane, F32),
                 pltpu.VMEM((group,) + plane, F32),
-                pltpu.VMEM(plane, F32),
                 pltpu.VMEM((slots, caps), jnp.int32),
                 pltpu.SMEM((slots,), jnp.int32),
                 pltpu.VMEM((caps, channels), F32),
                 pltpu.VMEM(target.shape, F32),
-                pltpu.VMEM(target.shape, F32),
                 pltpu.SemaphoreType.DMA((10,)),
-                pltpu.SemaphoreType.DMA((4,)),
                 pltpu.SemaphoreType.DMA((2 * steps, shots, 3)),
                 pltpu.SemaphoreType.DMA((2 * steps, shots, 3)),
                 pltpu.SemaphoreType.DMA((3, max(group - 1, 1))),
                 pltpu.SemaphoreType.DMA((3, max(group - 1, 1))),
             ],
             compiler_params=pltpu.CompilerParams(
-                collective_id=0, has_side_effects=True, vmem_limit_bytes=62 * 1024 * 1024
+                collective_id=0, has_side_effects=True, vmem_limit_bytes=48 * 1024 * 1024
             ),
         )(
-            pressure_init,
-            adjoint_init,
-            density,
-            speed,
-            admittance,
-            bound_mask,
-            rec_cells,
-            rec_live,
-            encoder,
-            target,
-        )
-        gradient = -(bound_mask.astype(F32) * total)
-        return record, gradient
+            in_hbm(pressure_init),
+            in_hbm(adjoint_init),
+            in_hbm(density),
+            in_hbm(speed),
+            in_hbm(admittance),
+            in_hbm(bound_mask),
+            in_hbm(rec_cells),
+            in_hbm(rec_live),
+            in_hbm(encoder),
+            in_hbm(target),
+        )
+        return pl.pallas_call(
+            deliver,
+            out_shape=(
+                jax.ShapeDtypeStruct(target.shape, F32),
+                jax.ShapeDtypeStruct(plane, F32),
+            ),
+            in_specs=[vmem_spec] * 2,
+            out_specs=(any_spec, any_spec),
+            scratch_shapes=[pltpu.SemaphoreType.DMA((2,))],
+        )(
+            pltpu.with_memory_space_constraint(record, pltpu.VMEM),
+            pltpu.with_memory_space_constraint(total, pltpu.VMEM),
+        )
 
     placed = (
         P("shot", "slab", None, None),

time: 22.2 us -> 19.9 us (0.90)
  the two profiles are of different devices: /device:TPU:25 before, /device:TPU:0 now
where the time goes in v3:
time: 19.9 us; the launch traced here: 19.7 us
  Pallas kernels  19.1 us (96%)
  between operations  0.64 us (3%)
    pallas_call x1, Pallas kernels, body(): pl.pallas_call(functools.partial(kernel, slabs, group, steps, slots), out...  18.3 us
    pallas_call x1, Pallas kernels, body(): pl.pallas_call(deliver, out_shape=(jax.ShapeDtypeStruct(target.shape, F32...  0.72 us

profile of v3, /device:TPU:0, one launch (start us, length us, event | category | flops | bytes accessed | tf_op | source)
XLA Modules:
  0.0 19.7 jit_solution(15718862786201388784)
XLA Ops:
  0.6 18.3 %shard_map.113 = (f32[3,2,2,25]{3,2,1,0:T(2,128)S(1)}, f32[8,32,256]{2,1,0:T(8,128)S(1)}) custom-call(f32[2,8,32,256]{3,2,1,0:T(8,128)} %pressure_hbm.1, f32[2,8,32,256]{3,2,1,0:T(8,128)} %adjoint_hbm.1, f32[8,32,256]{2,1,0:T(8,128)} %density_hbm.1, f32[8,32,256]{2,1,0:T(8,128)} %speed_hbm.1, f32[8,32,256]{2,1,0:T(8,128)} %admittance_hbm.1, ...), custom_call_target="tpu_custom_call" | custom-call | tf_op jit(solution)/shard_map/pallas_call | solution.py:517
  19.0 0.7 %shard_map.114 = (f32[3,2,2,25]{3,2,1,0:T(2,128)}, f32[8,32,256]{2,1,0:T(8,128)}) custom-call(f32[3,2,2,25]{3,2,1,0:T(2,128)S(1)} %get-tuple-element.4.record, f32[8,32,256]{2,1,0:T(8,128)S(1)} %get-tuple-element.5.total), custom_call_target="tpu_custom_call" | custom-call | tf_op jit(solution)/shard_map/pallas_call | solution.py:568

commit v4 on v3

--- a/solution.py
+++ b/solution.py
@@ -50,6 +50,8 @@
     after,
     placed,
     grads,
+    cross_out,
+    cross_in,
     cells,
     live,
     encoder,
@@ -59,6 +61,8 @@
     recv_sem,
     gsend_sem,
     grecv_sem,
+    rho_sem,
+    cross_sem,
 ):
     shots, depth, width_x, width_y = pressure_hbm.shape
     me = lax.axis_index("slab")
@@ -154,18 +158,43 @@
     rounds = [[halo(0, s, pressure_hbm, fields.at[0], 0, depth - 1) for s in each]]
     for n in range(1, steps):
         rounds.append([halo(n, s, fields.at[n], fields.at[n], 1, depth) for s in each])
-    for k in range(steps - 1):
+    for k in range(steps - 2):
         rounds.append(
             [halo(steps + k, s, weights.at[k], weights.at[k], 1, depth) for s in each]
         )
+    shared = group > 1 and width_x % (8 * group) == 0
+    size_x = width_x // group if shared else width_x
+    share_x = pl.ds(pl.multiple_of(mine * size_x, 8), size_x) if shared else pl.ds(0, size_x)
     density_up = pltpu.make_async_remote_copy(
-        src_ref=density_hbm.at[pl.ds(depth - 1, 1)],
-        dst_ref=density.at[pl.ds(0, 1)],
+        src_ref=density_hbm.at[depth - 1, share_x],
+        dst_ref=density.at[0, share_x],
         send_sem=send_sem.at[0, 0, 2],
         recv_sem=recv_sem.at[0, 0, 2],
         device_id={"slab": me + 1},
         device_id_type=MESH,
     )
+    density_swap = [
+        pltpu.make_async_remote_copy(
+            src_ref=density.at[0, share_x],
+            dst_ref=density.at[0, share_x],
+            send_sem=rho_sem.at[0, j - 1],
+            recv_sem=rho_sem.at[1, j - 1],
+            device_id={"shot": lax.rem(mine + j, group)},
+            device_id_type=MESH,
+        )
+        for j in range(1, group if shared else 1)
+    ]
+    cross = tuple(
+        pltpu.make_async_remote_copy(
+            src_ref=cross_out.at[i],
+            dst_ref=cross_in.at[i],
+            send_sem=cross_sem.at[0, i],
+            recv_sem=cross_sem.at[1, i],
+            device_id={"slab": me + 2 * i - 1},
+            device_id_type=MESH,
+        )
+        for i in range(2)
+    )
 
     pl.semaphore_wait(
         barrier, has_below.astype(jnp.int32) + has_above.astype(jnp.int32) + (group - 1)
@@ -183,17 +212,23 @@
     @pl.when(jnp.logical_not(has_below))
     def _():
         vel[0] = jnp.zeros((width_x, width_y), F32)
+        cross_in[1] = jnp.zeros((width_x, width_y), F32)
         for n in range(steps):
             fields[n, :, 0] = zero
-        for k in range(steps - 1):
+        for k in range(steps - 2):
             weights[k, :, 0] = zero
 
     @pl.when(jnp.logical_not(has_above))
     def _():
+        cross_in[0] = jnp.zeros((width_x, width_y), F32)
         for n in range(steps):
             fields[n, :, depth + 1] = zero
-        for k in range(steps - 1):
+        for k in range(steps - 2):
             weights[k, :, depth + 1] = zero
+
+    if steps > 1:
+        weights[steps - 2, :, 0] = zero
+        weights[steps - 2, :, depth + 1] = zero
 
     rows = lax.broadcasted_iota(jnp.int32, (width_x, width_y), 0)
     cols = lax.broadcasted_iota(jnp.int32, (width_x, width_y), 1)
@@ -335,16 +370,21 @@
             ]
         )
 
-    def sample(n, s, planes):
-        values = jnp.concatenate([after[n, s, z - 1] for z in planes], axis=0)
+    def sample(n, planes):
+        values = jnp.concatenate([after[n, s, z - 1] for s in each for z in planes], axis=0)
         got = jnp.dot(
             jnp.concatenate(split(values), axis=1), read_col, preferred_element_type=F32
         )
-        part = jnp.zeros((width_x, lanes), F32)
-        for i, z in enumerate(planes):
-            pick = band + (z - 1) * width_x == plane_at
-            part = part + jnp.where(pick, got[i * width_x : (i + 1) * width_x], 0.0)
-        return jnp.sum(part, axis=0, keepdims=True)
+        found = []
+        at = 0
+        for s in each:
+            part = jnp.zeros((width_x, lanes), F32)
+            for z in planes:
+                pick = band + (z - 1) * width_x == plane_at
+                part = part + jnp.where(pick, got[at : at + width_x], 0.0)
+                at += width_x
+            found.append(jnp.sum(part, axis=0, keepdims=True))
+        return found
 
     def encode(n, found):
         table = jnp.zeros((pad, lanes), F32)
@@ -356,58 +396,85 @@
                 i = r * shots + s
                 record[r, s, pl.ds(n, 1), :] = encoded[i : i + 1]
 
-    def source(n, s, found):
-        high, low = split(jnp.broadcast_to(found, (16, lanes)))
+    def source(n, found):
+        rows_of = lax.broadcasted_iota(jnp.int32, (-(-shots // 16) * 16, lanes), 0)
+        table = jnp.zeros(rows_of.shape, F32)
+        for s in each:
+            table = jnp.where(rows_of == s, found[s], table)
+        high, low = split(table)
         wide = jnp.dot(
             jnp.concatenate([high, low, high], axis=1), gram, preferred_element_type=F32
         )
-        return wide[0:1] * live_lane - goals[n][s]
-
-    def place(n, s, value, planes):
-        high, low = split(value)
-        both = jnp.concatenate([high.astype(F32), low.astype(F32)], axis=1)
+        return [wide[s : s + 1] * live_lane - goals[n][s] for s in each]
+
+    def place(n, values, planes):
         spots = []
-        for z in planes:
-            pick = band_twice + (z - 1) * width_x == plane_twice
-            spots.append(jnp.where(pick, both, 0.0).astype(jnp.bfloat16))
+        for s in each:
+            high, low = split(values[s])
+            both = jnp.concatenate([high.astype(F32), low.astype(F32)], axis=1)
+            for z in planes:
+                pick = band_twice + (z - 1) * width_x == plane_twice
+                spots.append(jnp.where(pick, both, 0.0).astype(jnp.bfloat16))
         put = lax.dot_general(
             jnp.concatenate(spots, axis=0),
             write_col,
             (((1,), (1,)), ((), ())),
             preferred_element_type=F32,
         )
-        for i, z in enumerate(planes):
-            placed[n, s, z - 1] = put[i * width_x : (i + 1) * width_x]
+        at = 0
+        for s in each:
+            for z in planes:
+                placed[n, s, z - 1] = put[at : at + width_x]
+                at += width_x
+
+    @pl.when(has_below)
+    def _():
+        density_up.wait_recv()
+        for copy in density_swap:
+            copy.start()
 
     last = steps - 1
     for n in range(steps):
         over(2, depth, functools.partial(forward, n, each))
         if n == last:
-            found = [sample(n, s, middle) for s in each]
+            found = sample(n, middle)
             loads[9].wait()
         if n == 0:
 
             @pl.when(has_below)
             def _():
-                density_up.wait_recv()
+                for copy in density_swap:
+                    copy.wait_recv()
                 vel[0] = 0.5 / density[0]
                 add_below(1)
 
-        sources = []
         for s in each:
             arrive(rounds[n][s])
             for z in edges:
                 forward(n, (s,), z)
             if n < last:
                 start(rounds[n + 1][s])
-            else:
-                found[s] = found[s] + sample(n, s, edges)
-                sources.append(source(n, s, found[s]))
-                place(n, s, sources[s], edges)
-                for z in edges:
-                    backward(n, (s,), z)
-                if n > 0:
-                    start(rounds[steps][s])
+
+    found = [a + b for a, b in zip(found, sample(last, edges))]
+    sources = source(last, found)
+    place(last, sources, edges)
+    for z in edges:
+        backward(last, each, z)
+
+    def send_cross():
+        for i, (z, beyond) in enumerate(((1, 0), (depth, depth + 1))):
+            part = None
+            for s in each:
+                term = weights[steps - 2, s, z] * (fields[1, s, beyond] - fields[0, s, beyond])
+                part = term if part is None else part + term
+            cross_out[i] = part
+        start(cross)
+
+    if last > 1:
+        for s in each:
+            start(rounds[steps][s])
+    elif last == 1:
+        send_cross()
 
     def share(k, low, size):
         planes = pl.ds(low, size)
@@ -428,29 +495,34 @@
     parts = [(1, depth - 2), (0, 1), (depth - 1, 1)]
     shares = [share(k, low, size) for k, (low, size) in enumerate(parts)]
 
-    for s in each:
-        place(last, s, sources[s], middle)
+    place(last, sources, middle)
     over(2, depth, functools.partial(backward, last, each))
     for n in reversed(range(last)):
         k = last - n
-        old = [sample(n, s, middle + edges) for s in each]
-        for s in each:
-            place(n, s, source(n, s, old[s]), middle + edges)
-        over(2, depth, functools.partial(backward, n, each))
+        old = sample(n, middle + edges)
+        place(n, source(n, old), middle + edges)
         if n == 0:
+            over(1, depth + 1, functools.partial(backward, n, each))
             for copy in shares[0]:
                 copy.start()
+        else:
+            over(2, depth, functools.partial(backward, n, each))
+            for s in each:
+                arrive(rounds[steps + k - 1][s])
+            for z in edges:
+                backward(n, each, z)
+            if n > 1:
+                for s in each:
+                    start(rounds[steps + k][s])
+            else:
+                send_cross()
         encode(n, old)
-        if n == 0:
-            encode(last, found)
-        for s in each:
-            arrive(rounds[steps + k - 1][s])
-            for z in edges:
-                backward(n, (s,), z)
-            if n > 0:
-                start(rounds[steps + k][s])
-    if steps == 1:
-        encode(last, found)
+    encode(last, found)
+    if last > 0:
+        arrive(cross)
+        for i, (z, face) in enumerate(((depth, depth), (1, 0))):
+            grads[mine, z - 1] = grads[mine, z - 1] + vel[face] / damp[z - 1] * cross_in[i]
+    else:
         for copy in shares[0]:
             copy.start()
     for copy in shares[1] + shares[2]:
@@ -468,9 +540,17 @@
         for pair in pairs:
             sent(pair)
 
+    if last > 0:
+        sent(cross)
+
     @pl.when(has_above)
     def _():
         density_up.wait_send()
+
+    @pl.when(has_below)
+    def _():
+        for copy in density_swap:
+            copy.wait_send()
 
     for copies in shares:
         for copy in copies:
@@ -540,6 +620,8 @@
                 pltpu.VMEM((steps, shots) + plane, F32),
                 pltpu.VMEM((steps, shots) + plane, F32),
                 pltpu.VMEM((group,) + plane, F32),
+                pltpu.VMEM((2, width_x, width_y), F32),
+                pltpu.VMEM((2, width_x, width_y), F32),
                 pltpu.VMEM((slots, caps), jnp.int32),
                 pltpu.SMEM((slots,), jnp.int32),
                 pltpu.VMEM((caps, channels), F32),
@@ -549,6 +631,8 @@
                 pltpu.SemaphoreType.DMA((2 * steps, shots, 3)),
                 pltpu.SemaphoreType.DMA((3, max(group - 1, 1))),
                 pltpu.SemaphoreType.DMA((3, max(group - 1, 1))),
+                pltpu.SemaphoreType.DMA((2, max(group - 1, 1))),
+                pltpu.SemaphoreType.DMA((2, 2)),
             ],
             compiler_params=pltpu.CompilerParams(
                 collective_id=0, has_side_effects=True, vmem_limit_bytes=48 * 1024 * 1024

time: 19.9 us -> 19.6 us (0.985)
  Pallas kernels: 19.1 us -> 18.8 us
    pallas_call x1, Pallas kernels: 18.3 us -> 18.1 us  [body(): pl.pallas_call(functools.partial(kernel, slabs, group, steps, slots), out...]
where the time goes in v4:
time: 19.6 us; the launch traced here: 19.5 us
  Pallas kernels  18.8 us (96%)
  between operations  0.64 us (3%)
    pallas_call x1, Pallas kernels, body(): pl.pallas_call(functools.partial(kernel, slabs, group, steps, slots), out...  18.1 us
    pallas_call x1, Pallas kernels, body(): pl.pallas_call(deliver, out_shape=(jax.ShapeDtypeStruct(target.shape, F32...  0.72 us

profile of v4, /device:TPU:0, one launch (start us, length us, event | category | flops | bytes accessed | tf_op | source)
XLA Modules:
  0.0 19.5 jit_solution(6478632144900928442)
XLA Ops:
  0.6 18.1 %shard_map.113 = (f32[3,2,2,25]{3,2,1,0:T(2,128)S(1)}, f32[8,32,256]{2,1,0:T(8,128)S(1)}) custom-call(f32[2,8,32,256]{3,2,1,0:T(8,128)} %pressure_hbm.1, f32[2,8,32,256]{3,2,1,0:T(8,128)} %adjoint_hbm.1, f32[8,32,256]{2,1,0:T(8,128)} %density_hbm.1, f32[8,32,256]{2,1,0:T(8,128)} %speed_hbm.1, f32[8,32,256]{2,1,0:T(8,128)} %admittance_hbm.1, ...), custom_call_target="tpu_custom_call" | custom-call | tf_op jit(solution)/shard_map/pallas_call | solution.py:597
  18.8 0.7 %shard_map.114 = (f32[3,2,2,25]{3,2,1,0:T(2,128)}, f32[8,32,256]{2,1,0:T(8,128)}) custom-call(f32[3,2,2,25]{3,2,1,0:T(2,128)S(1)} %get-tuple-element.4.record, f32[8,32,256]{2,1,0:T(8,128)S(1)} %get-tuple-element.5.total), custom_call_target="tpu_custom_call" | custom-call | tf_op jit(solution)/shard_map/pallas_call | solution.py:652

commit v5 on v4

--- a/solution.py
+++ b/solution.py
@@ -52,6 +52,9 @@
     grads,
     cross_out,
     cross_in,
+    early,
+    coef_out,
+    coef_in,
     cells,
     live,
     encoder,
@@ -61,7 +64,8 @@
     recv_sem,
     gsend_sem,
     grecv_sem,
-    rho_sem,
+    swap_sem,
+    coef_sem,
     cross_sem,
 ):
     shots, depth, width_x, width_y = pressure_hbm.shape
@@ -70,13 +74,28 @@
     has_below = me > 0
     has_above = me < slabs - 1
 
+    barrier = pltpu.get_barrier_semaphore()
+
+    @pl.when(has_below)
+    def _():
+        pl.semaphore_signal(barrier, inc=1, device_id={"slab": me - 1}, device_id_type=MESH)
+
+    @pl.when(has_above)
+    def _():
+        pl.semaphore_signal(barrier, inc=1, device_id={"slab": me + 1}, device_id_type=MESH)
+
+    for j in range(1, group):
+        pl.semaphore_signal(
+            barrier, inc=1, device_id={"shot": lax.rem(mine + j, group)}, device_id_type=MESH
+        )
+
     inner = pl.ds(1, depth)
     pairs = [
+        (pressure_hbm, fields.at[0, :, inner]),
         (density_hbm, density.at[inner]),
         (speed_hbm, pres),
         (admittance_hbm, damp),
         (mask_hbm, mask),
-        (pressure_hbm, fields.at[0, :, inner]),
         (cells_hbm, cells),
         (live_hbm, live),
         (encoder_hbm, encoder),
@@ -87,21 +106,6 @@
     for load in loads:
         load.start()
 
-    barrier = pltpu.get_barrier_semaphore()
-
-    @pl.when(has_below)
-    def _():
-        pl.semaphore_signal(barrier, inc=1, device_id={"slab": me - 1}, device_id_type=MESH)
-
-    @pl.when(has_above)
-    def _():
-        pl.semaphore_signal(barrier, inc=1, device_id={"slab": me + 1}, device_id_type=MESH)
-
-    for j in range(1, group):
-        pl.semaphore_signal(
-            barrier, inc=1, device_id={"shot": lax.rem(mine + j, group)}, device_id_type=MESH
-        )
-
     def halo(k, s, source, into, first, last):
         down = pltpu.make_async_remote_copy(
             src_ref=source.at[s, pl.ds(first, 1)],
@@ -155,8 +159,10 @@
             up.wait_send()
 
     each = range(shots)
-    rounds = [[halo(0, s, pressure_hbm, fields.at[0], 0, depth - 1) for s in each]]
-    for n in range(1, steps):
+    rounds = [[halo(0, s, fields.at[0], fields.at[0], 1, depth) for s in each]]
+    if steps > 1:
+        rounds.append([halo(1, s, early, fields.at[1], 0, 1) for s in each])
+    for n in range(2, steps):
         rounds.append([halo(n, s, fields.at[n], fields.at[n], 1, depth) for s in each])
     for k in range(steps - 2):
         rounds.append(
@@ -165,22 +171,29 @@
     shared = group > 1 and width_x % (8 * group) == 0
     size_x = width_x // group if shared else width_x
     share_x = pl.ds(pl.multiple_of(mine * size_x, 8), size_x) if shared else pl.ds(0, size_x)
-    density_up = pltpu.make_async_remote_copy(
-        src_ref=density_hbm.at[depth - 1, share_x],
-        dst_ref=density.at[0, share_x],
-        send_sem=send_sem.at[0, 0, 2],
-        recv_sem=recv_sem.at[0, 0, 2],
-        device_id={"slab": me + 1},
-        device_id_type=MESH,
+    coef_parts = (pl.ds(0, 1), pl.ds(1, 2))
+    coefs = tuple(
+        pltpu.make_async_remote_copy(
+            src_ref=coef_out.at[coef_parts[i], share_x],
+            dst_ref=coef_in.at[coef_parts[i], share_x],
+            send_sem=coef_sem.at[0, i],
+            recv_sem=coef_sem.at[1, i],
+            device_id={"slab": me + 2 * i - 1},
+            device_id_type=MESH,
+        )
+        for i in range(2)
     )
-    density_swap = [
-        pltpu.make_async_remote_copy(
-            src_ref=density.at[0, share_x],
-            dst_ref=density.at[0, share_x],
-            send_sem=rho_sem.at[0, j - 1],
-            recv_sem=rho_sem.at[1, j - 1],
-            device_id={"shot": lax.rem(mine + j, group)},
-            device_id_type=MESH,
+    swaps = [
+        tuple(
+            pltpu.make_async_remote_copy(
+                src_ref=coef_in.at[coef_parts[i], share_x],
+                dst_ref=coef_in.at[coef_parts[i], share_x],
+                send_sem=swap_sem.at[0, i, j - 1],
+                recv_sem=swap_sem.at[1, i, j - 1],
+                device_id={"shot": lax.rem(mine + j, group)},
+                device_id_type=MESH,
+            )
+            for i in range(2)
         )
         for j in range(1, group if shared else 1)
     ]
@@ -196,17 +209,6 @@
         for i in range(2)
     )
 
-    pl.semaphore_wait(
-        barrier, has_below.astype(jnp.int32) + has_above.astype(jnp.int32) + (group - 1)
-    )
-
-    @pl.when(has_above)
-    def _():
-        density_up.start()
-
-    for s in each:
-        start(rounds[0][s])
-
     zero = jnp.zeros((shots, width_x, width_y), F32)
 
     @pl.when(jnp.logical_not(has_below))
@@ -233,12 +235,15 @@
     rows = lax.broadcasted_iota(jnp.int32, (width_x, width_y), 0)
     cols = lax.broadcasted_iota(jnp.int32, (width_x, width_y), 1)
 
+    def level(q, z):
+        along_x = next_x[z] * pltpu.roll(q, width_x - 1, 0) + prev_x[z] * pltpu.roll(q, 1, 0)
+        along_y = next_y[z] * pltpu.roll(q, width_y - 1, 1) + prev_y[z] * pltpu.roll(q, 1, 1)
+        return along_x + along_y
+
     def spread(ref, n, s, z):
         q = ref[n, s, z]
-        along_x = next_x[z] * pltpu.roll(q, width_x - 1, 0) + prev_x[z] * pltpu.roll(q, 1, 0)
-        along_y = next_y[z] * pltpu.roll(q, width_y - 1, 1) + prev_y[z] * pltpu.roll(q, 1, 1)
         along_z = vel[z] * ref[n, s, z + 1] + vel[z - 1] * ref[n, s, z - 1]
-        return (along_x + along_y) + (along_z - centre[z] * q)
+        return level(q, z) + (along_z - centre[z] * q)
 
     def forward(n, which, z):
         for s in which:
@@ -281,7 +286,7 @@
     edges = (1, depth)
     middle = tuple(range(2, depth))
 
-    for load in loads[:4]:
+    for load in loads[:5]:
         load.wait()
 
     def coefficients(z):
@@ -304,7 +309,25 @@
 
     over(1, depth + 1, coefficients)
     over(2, depth + 1, add_below)
-    for load in loads[4:9]:
+    for i, z in enumerate(edges):
+        coef_out[i] = damp[z - 1] * pres[z - 1]
+    coef_out[2] = vel[depth]
+
+    pl.semaphore_wait(
+        barrier, has_below.astype(jnp.int32) + has_above.astype(jnp.int32) + (group - 1)
+    )
+    start(coefs)
+    for s in each:
+        start(rounds[0][s])
+    if steps > 1:
+        for s in each:
+            for i, (z, beside) in enumerate(((1, 2), (depth, depth - 1))):
+                q = fields[0, s, z]
+                near = level(q, z) + vel[min(z, beside)] * fields[0, s, beside] - centre[z] * q
+                early[s, i] = q + (q + pres[z - 1] * near) * damp[z - 1]
+            start(rounds[1][s])
+
+    for load in loads[5:9]:
         load.wait()
 
     caps, channels = encoder.shape
@@ -427,12 +450,6 @@
                 placed[n, s, z - 1] = put[at : at + width_x]
                 at += width_x
 
-    @pl.when(has_below)
-    def _():
-        density_up.wait_recv()
-        for copy in density_swap:
-            copy.start()
-
     last = steps - 1
     for n in range(steps):
         over(2, depth, functools.partial(forward, n, each))
@@ -440,19 +457,48 @@
             found = sample(n, middle)
             loads[9].wait()
         if n == 0:
+            arrive(coefs)
+
+            @pl.when(has_above)
+            def _():
+                for pair in swaps:
+                    pair[0].start()
 
             @pl.when(has_below)
             def _():
-                for copy in density_swap:
-                    copy.wait_recv()
-                vel[0] = 0.5 / density[0]
+                for pair in swaps:
+                    pair[1].start()
+
+            for pair in swaps:
+                arrive(pair)
+
+            @pl.when(has_below)
+            def _():
+                vel[0] = coef_in[2]
                 add_below(1)
 
         for s in each:
             arrive(rounds[n][s])
-            for z in edges:
-                forward(n, (s,), z)
-            if n < last:
+        if n == 1:
+
+            @pl.when(has_above)
+            def _():
+                rate = coef_in[0] * vel[depth]
+                for s in each:
+                    fields[1, s, depth + 1] = fields[1, s, depth + 1] + rate * (
+                        fields[0, s, depth] - fields[0, s, depth + 1]
+                    )
+
+            @pl.when(has_below)
+            def _():
+                rate = coef_in[1] * vel[0]
+                for s in each:
+                    fields[1, s, 0] = fields[1, s, 0] + rate * fields[0, s, 1]
+
+        for z in edges:
+            forward(n, each, z)
+        if 0 < n < last:
+            for s in each:
                 start(rounds[n + 1][s])
 
     found = [a + b for a, b in zip(found, sample(last, edges))]
@@ -519,9 +565,10 @@
         encode(n, old)
     encode(last, found)
     if last > 0:
+        ratios = [vel[face] / damp[z - 1] for z, face in ((depth, depth), (1, 0))]
         arrive(cross)
-        for i, (z, face) in enumerate(((depth, depth), (1, 0))):
-            grads[mine, z - 1] = grads[mine, z - 1] + vel[face] / damp[z - 1] * cross_in[i]
+        for i, z in enumerate((depth, 1)):
+            grads[mine, z - 1] = grads[mine, z - 1] + ratios[i] * cross_in[i]
     else:
         for copy in shares[0]:
             copy.start()
@@ -542,15 +589,17 @@
 
     if last > 0:
         sent(cross)
+    sent(coefs)
 
     @pl.when(has_above)
     def _():
-        density_up.wait_send()
+        for pair in swaps:
+            pair[0].wait_send()
 
     @pl.when(has_below)
     def _():
-        for copy in density_swap:
-            copy.wait_send()
+        for pair in swaps:
+            pair[1].wait_send()
 
     for copies in shares:
         for copy in copies:
@@ -622,6 +671,9 @@
                 pltpu.VMEM((group,) + plane, F32),
                 pltpu.VMEM((2, width_x, width_y), F32),
                 pltpu.VMEM((2, width_x, width_y), F32),
+                pltpu.VMEM((shots, 2, width_x, width_y), F32),
+                pltpu.VMEM((3, width_x, width_y), F32),
+                pltpu.VMEM((3, width_x, width_y), F32),
                 pltpu.VMEM((slots, caps), jnp.int32),
                 pltpu.SMEM((slots,), jnp.int32),
                 pltpu.VMEM((caps, channels), F32),
@@ -631,7 +683,8 @@
                 pltpu.SemaphoreType.DMA((2 * steps, shots, 3)),
                 pltpu.SemaphoreType.DMA((3, max(group - 1, 1))),
                 pltpu.SemaphoreType.DMA((3, max(group - 1, 1))),
-                pltpu.SemaphoreType.DMA((2, max(group - 1, 1))),
+                pltpu.SemaphoreType.DMA((2, 2, max(group - 1, 1))),
+                pltpu.SemaphoreType.DMA((2, 2)),
                 pltpu.SemaphoreType.DMA((2, 2)),
             ],
             compiler_params=pltpu.CompilerParams(

time: 19.6 us -> 18.9 us (0.964)
  Pallas kernels: 18.8 us -> 18.1 us
    pallas_call x1, Pallas kernels: 18.1 us -> 17.4 us  [body(): pl.pallas_call(functools.partial(kernel, slabs, group, steps, slots), out...]
where the time goes in v5:
time: 18.9 us; the launch traced here: 18.7 us
  Pallas kernels  18.1 us (96%)
  between operations  0.64 us (3%)
    pallas_call x1, Pallas kernels, body(): pl.pallas_call(functools.partial(kernel, slabs, group, steps, slots), out...  17.4 us
    pallas_call x1, Pallas kernels, body(): pl.pallas_call(deliver, out_shape=(jax.ShapeDtypeStruct(target.shape, F32...  0.72 us

profile of v5, /device:TPU:0, one launch (start us, length us, event | category | flops | bytes accessed | tf_op | source)
XLA Modules:
  0.0 18.7 jit_solution(15449395013318982142)
XLA Ops:
  0.6 17.4 %shard_map.113 = (f32[3,2,2,25]{3,2,1,0:T(2,128)S(1)}, f32[8,32,256]{2,1,0:T(8,128)S(1)}) custom-call(f32[2,8,32,256]{3,2,1,0:T(8,128)} %pressure_hbm.1, f32[2,8,32,256]{3,2,1,0:T(8,128)} %adjoint_hbm.1, f32[8,32,256]{2,1,0:T(8,128)} %density_hbm.1, f32[8,32,256]{2,1,0:T(8,128)} %speed_hbm.1, f32[8,32,256]{2,1,0:T(8,128)} %admittance_hbm.1, ...), custom_call_target="tpu_custom_call" | custom-call | tf_op jit(solution)/shard_map/pallas_call | solution.py:646
  18.0 0.7 %shard_map.114 = (f32[3,2,2,25]{3,2,1,0:T(2,128)}, f32[8,32,256]{2,1,0:T(8,128)}) custom-call(f32[3,2,2,25]{3,2,1,0:T(2,128)S(1)} %get-tuple-element.4.record, f32[8,32,256]{2,1,0:T(8,128)S(1)} %get-tuple-element.5.total), custom_call_target="tpu_custom_call" | custom-call | tf_op jit(solution)/shard_map/pallas_call | solution.py:705

commit v6 on v5

--- a/solution.py
+++ b/solution.py
@@ -455,6 +455,10 @@
         over(2, depth, functools.partial(forward, n, each))
         if n == last:
             found = sample(n, middle)
+            olds = []
+            for m in range(last):
+                olds.append(sample(m, middle + edges))
+                place(m, source(m, olds[m]), middle + edges)
             loads[9].wait()
         if n == 0:
             arrive(coefs)
@@ -545,8 +549,6 @@
     over(2, depth, functools.partial(backward, last, each))
     for n in reversed(range(last)):
         k = last - n
-        old = sample(n, middle + edges)
-        place(n, source(n, old), middle + edges)
         if n == 0:
             over(1, depth + 1, functools.partial(backward, n, each))
             for copy in shares[0]:
@@ -562,18 +564,19 @@
                     start(rounds[steps + k][s])
             else:
                 send_cross()
-        encode(n, old)
+        encode(n, olds[n])
     encode(last, found)
     if last > 0:
         ratios = [vel[face] / damp[z - 1] for z, face in ((depth, depth), (1, 0))]
-        arrive(cross)
         for i, z in enumerate((depth, 1)):
+            pl.when(has_below if i else has_above)(cross[i].wait_recv)
             grads[mine, z - 1] = grads[mine, z - 1] + ratios[i] * cross_in[i]
+            for copy in shares[2 - i]:
+                copy.start()
     else:
-        for copy in shares[0]:
-            copy.start()
-    for copy in shares[1] + shares[2]:
-        copy.start()
+        for copies in shares:
+            for copy in copies:
+                copy.start()
 
     for k, (low, size) in enumerate(parts):
         for copy in shares[k]:

time: 18.9 us -> 18.9 us (level)
  no operation moved by 1% of the time
where the time goes in v6:
time: 18.9 us; the launch traced here: 18.7 us
  Pallas kernels  18.1 us (96%)
  between operations  0.64 us (3%)
    pallas_call x1, Pallas kernels, body(): pl.pallas_call(functools.partial(kernel, slabs, group, steps, slots), out...  17.3 us
    pallas_call x1, Pallas kernels, body(): pl.pallas_call(deliver, out_shape=(jax.ShapeDtypeStruct(target.shape, F32...  0.72 us

profile of v6, /device:TPU:0, one launch (start us, length us, event | category | flops | bytes accessed | tf_op | source)
XLA Modules:
  0.0 18.7 jit_solution(14624057049833284579)
XLA Ops:
  0.6 17.3 %shard_map.113 = (f32[3,2,2,25]{3,2,1,0:T(2,128)S(1)}, f32[8,32,256]{2,1,0:T(8,128)S(1)}) custom-call(f32[2,8,32,256]{3,2,1,0:T(8,128)} %pressure_hbm.1, f32[2,8,32,256]{3,2,1,0:T(8,128)} %adjoint_hbm.1, f32[8,32,256]{2,1,0:T(8,128)} %density_hbm.1, f32[8,32,256]{2,1,0:T(8,128)} %speed_hbm.1, f32[8,32,256]{2,1,0:T(8,128)} %admittance_hbm.1, ...), custom_call_target="tpu_custom_call" | custom-call | tf_op jit(solution)/shard_map/pallas_call | solution.py:649
  18.0 0.7 %shard_map.114 = (f32[3,2,2,25]{3,2,1,0:T(2,128)}, f32[8,32,256]{2,1,0:T(8,128)}) custom-call(f32[3,2,2,25]{3,2,1,0:T(2,128)S(1)} %get-tuple-element.4.record, f32[8,32,256]{2,1,0:T(8,128)S(1)} %get-tuple-element.5.total), custom_call_target="tpu_custom_call" | custom-call | tf_op jit(solution)/shard_map/pallas_call | solution.py:708
